TPU v7x, 256 devices: a whole 4x4x8 slice. The times are simulated.
256 devices in a mesh: tile: 64 (over x_lo, y, z), mode: 4 (over x_hi, core).
Axes of the slice: x: 4 (x_hi: 2, x_lo: 2; x = x_hi * 2 + x_lo), y: 4, z: 8, core: 2. Of those that a mesh axis runs over, the one named last changes fastest.
Arguments:
- object_field: float32 [2, 512, 32768], P(None, 'mode', 'tile'), may hold values from -5 to 5
- probe: float32 [8, 2, 256, 256], P('mode'), may hold values from -1.5 to 1.5
- measured: float32 [768, 256, 256], P(('tile', 'mode')), may hold values from 0.3 to 3
- scan_rows: int32 [768], P(('tile', 'mode')), may hold values from 0 to 256
- scan_cols: int32 [768], P(('tile', 'mode')), may hold values from 0 to 512
- counts: int32 [64], P('tile'), may hold values from 1 to 12, 240 in all
Outputs:
- object_out: float32 [2, 512, 32768], P(None, 'mode', 'tile')
- probe_out: float32 [8, 2, 256, 256], P('mode', None, 'tile')
Inputs may be any that keep to these rules, and one draw needn't show every extreme that they name: Slot j of tile t holds a scan exactly when j < counts[t]; some tile has all 12 slots live.
All inputs are finite; a program needn't handle non-finite values. No bound on the sum of `counts` on one device may be relied on, other than what follows from the above.
Results may differ from a plain program's by a relative error of at most 0.0014.
Values may be sent and summed in bfloat16 or wider, within the bound.
A program may use at most 128 MiB of HBM per device.

v0:
```python
import jax
import jax.numpy as jnp
from jax import lax
from jax.sharding import PartitionSpec as P

object_reg = 0.5
probe_reg = 1.0
power_floor = 0.25


def extended_2(array, sides, width):
    for axis, dim in sides:
        peers, length = (lax.axis_size(axis), array.shape[dim])
        up = [(i, (i + 1) % peers) for i in range(peers - 1)]
        down = [(j, i) for i, j in up]
        last = lax.slice_in_dim(array, length - width, length, axis=dim)
        leading = lax.slice_in_dim(array, 0, width, axis=dim)
        before = lax.ppermute(last, axis, up)
        after = lax.ppermute(leading, axis, down)
        array = jnp.concatenate([before, array, after], axis=dim)
    return array


def passed_along(block, axis, distance):
    devices = range(lax.axis_size(axis))
    route = [(i - distance, i) for i in devices if i - distance in devices]
    return lax.ppermute(block, axis, route)


def dft_blocks(length):
    positions = jnp.arange(length, dtype=jnp.int32)
    product = positions[:, None] * positions[None, :] % length
    angles = product.astype(jnp.float32) * (2.0 * jnp.pi / length)
    scaling = 1.0 / jnp.sqrt(jnp.float32(length))
    real_part = (jnp.cos(angles) * scaling).astype(jnp.bfloat16)
    imag_part = (-jnp.sin(angles) * scaling).astype(jnp.bfloat16)
    forward = jnp.concatenate(
        [jnp.concatenate([real_part, imag_part], 1), jnp.concatenate([-imag_part, real_part], 1)], 0
    )
    inverse = jnp.concatenate(
        [jnp.concatenate([real_part, -imag_part], 1), jnp.concatenate([imag_part, real_part], 1)], 0
    )
    return (forward, inverse)


def along_last(values, matrix):
    flattened = values.reshape(values.shape[0] * values.shape[1], values.shape[2])
    result = jnp.dot(flattened, matrix, preferred_element_type=jnp.float32)
    return result.reshape(values.shape[0], values.shape[1], matrix.shape[1])


def swap_axes(values):
    batch_count, length, doubled = values.shape
    half_width = doubled // 2
    return (
        values.reshape(batch_count, length, 2, half_width)
        .transpose(0, 3, 2, 1)
        .reshape(batch_count, half_width, 2 * length)
    )


def correction(object_patch, probe_half, amplitude, forward, inverse):
    length = amplitude.shape[0]
    patch_re = object_patch[0].astype(jnp.float32)
    patch_im = object_patch[1].astype(jnp.float32)
    probe_re = probe_half[:, 0].astype(jnp.float32)
    probe_im = probe_half[:, 1].astype(jnp.float32)
    wave = jnp.concatenate(
        [probe_re * patch_re - probe_im * patch_im, probe_re * patch_im + probe_im * patch_re], 2
    ).astype(jnp.bfloat16)
    half_spectrum = along_last(wave, forward).astype(jnp.bfloat16)
    spectrum = along_last(swap_axes(half_spectrum), forward)
    spec_re = spectrum[:, :, :length]
    spec_im = spectrum[:, :, length:]
    power_sum = jnp.sum(spec_re * spec_re + spec_im * spec_im, 0)
    factor = amplitude.T / jnp.sqrt(jnp.maximum(power_sum, power_floor)) - 1.0
    difference = (spectrum * jnp.concatenate([factor, factor], 1)[None]).astype(jnp.bfloat16)
    back_half = along_last(difference, inverse).astype(jnp.bfloat16)
    back = along_last(swap_axes(back_half), inverse)
    return (back[:, :, :length], back[:, :, length:])


def local(object_field, probe, measured, scan_rows, scan_cols, counts):
    modes_here = probe.shape[0]
    length = probe.shape[2]
    margin = length // 2
    tile_width = object_field.shape[2]
    groups = lax.axis_size("mode")
    tiles = lax.axis_size("tile")
    slots = scan_rows.shape[0]
    forward, inverse = dft_blocks(length)
    probe_half = probe.astype(jnp.bfloat16)
    object_half = object_field.astype(jnp.bfloat16)
    probe_all, object_rows = (
        lax.all_gather(probe_half, "mode", axis=0, tiled=True),
        lax.all_gather(object_half, "mode", axis=1, tiled=True),
    )
    extended = extended_2(object_rows, (("tile", 2),), margin)
    full_rows = extended.shape[1]
    probe_re = probe_all[:, 0].astype(jnp.float32)
    probe_im = probe_all[:, 1].astype(jnp.float32)
    lighting = jnp.sum(probe_re * probe_re + probe_im * probe_im, 0)
    first_slot = lax.axis_index("mode") * slots
    live_total = counts[0]

    def slot_step(slot_index, accumulated):
        gradient, probe_grad, weight_sum = accumulated
        live_flag = (first_slot + slot_index < live_total).astype(jnp.float32)
        row_start = scan_rows[slot_index]
        col_start = scan_cols[slot_index]
        object_patch = lax.dynamic_slice(extended, (0, row_start, col_start), (2, length, length))
        back_re, back_im = correction(
            object_patch, probe_all, measured[slot_index], forward, inverse
        )
        back_re = back_re * live_flag
        back_im = back_im * live_flag
        grad_re = jnp.sum(probe_re * back_re + probe_im * back_im, 0)
        grad_im = jnp.sum(probe_re * back_im - probe_im * back_re, 0)
        term = jnp.stack([grad_re, grad_im, lighting * live_flag])
        previous = lax.dynamic_slice(gradient, (0, row_start, col_start), (3, length, length))
        gradient = lax.dynamic_update_slice(gradient, previous + term, (0, row_start, col_start))
        patch_re = object_patch[0].astype(jnp.float32)
        patch_im = object_patch[1].astype(jnp.float32)
        term_re = patch_re * back_re + patch_im * back_im
        term_im = patch_re * back_im - patch_im * back_re
        probe_grad = probe_grad + jnp.stack([term_re, term_im], 1)
        weight_sum = weight_sum + (patch_re * patch_re + patch_im * patch_im) * live_flag
        return (gradient, probe_grad, weight_sum)

    initial = (
        jnp.zeros((3, full_rows, tile_width + length), jnp.float32),
        jnp.zeros((probe_all.shape[0], 2, length, length), jnp.float32),
        jnp.zeros((length, length), jnp.float32),
    )
    gradient, probe_grad, weight_sum = lax.fori_loop(0, slots, slot_step, initial)
    left_rim = gradient[:, :, :margin]
    right_rim = gradient[:, :, tile_width + margin :]
    central = gradient[:, :, margin : tile_width + margin]
    from_right = passed_along(left_rim, "tile", -1)
    from_left = passed_along(right_rim.astype(jnp.bfloat16), "tile", 1).astype(right_rim.dtype)
    central = central.at[:, :, tile_width - margin :].add(from_right)
    central = central.at[:, :, :margin].add(from_left)
    summed = lax.psum_scatter(central, "mode", scatter_dimension=1, tiled=True)
    object_out = object_field + summed[:2] / (summed[2] + object_reg)
    grouped = probe_grad.reshape(groups, 2 * modes_here, length, length)
    power_plane = weight_sum.reshape(1, 1, length, length)
    partial_sum, power_band = (
        lax.psum_scatter(grouped, "tile", scatter_dimension=2, tiled=True),
        lax.psum_scatter(power_plane, "tile", scatter_dimension=2, tiled=True),
    )
    owned = lax.psum_scatter(partial_sum, "mode", scatter_dimension=0, tiled=True)
    power_total = lax.psum(power_band, "mode")
    band_rows = length // tiles
    first_row = lax.axis_index("tile") * band_rows
    probe_rows = lax.dynamic_slice_in_dim(probe, first_row, band_rows, 2)
    steps_term = owned[0].reshape(modes_here, 2, band_rows, length)
    probe_out = probe_rows + steps_term / (power_total[0, 0] + probe_reg)
    return (object_out, probe_out)


def solution(mesh):
    return jax.shard_map(
        local,
        mesh=mesh,
        in_specs=(
            P(None, "mode", "tile"),
            P("mode", None, None, None),
            P(("tile", "mode"), None, None),
            P(("tile", "mode")),
            P(("tile", "mode")),
            P("tile"),
        ),
        out_specs=(P(None, "mode", "tile"), P("mode", None, "tile", None)),
        check_vma=False,
    )
```

profile of v0, /device:TPU:6, one launch (start us, length us, event | category | flops | bytes accessed | tf_op | source)
XLA Modules:
  0.0 1026.5 jit_solution(15595923657649589083)
XLA Ops:
  11.2 23.3 %all-gather.5.cloned.1.call-done = bf16[2,512,512]{2,1,0:T(8,128)(2,1)} async-done(((bf16[2,128,512]{2,1,0:T(8,128)(2,1)}), bf16[2,512,512]{2,1,0:T(8,128)(2,1)}) %all-gather.5.cloned.1.call-update) | async-done | bytes 1048592 | tf_op jit(solution)/shard_map/all_gather | solution.py:96
  35.7 3.5 collective-permute-start
  39.2 6.6 collective-permute-start.1
  52.8 12.8 %all-gather.3.cloned.1.call-done = bf16[8,2,256,256]{3,2,0,1:T(8,128)(2,1)} async-done(((bf16[2,2,256,256]{3,2,0,1:T(8,128)(2,1)}), bf16[8,2,256,256]{3,2,0,1:T(8,128)(2,1)}) %all-gather.3.cloned.1.call-update) | async-done | bytes 2097168 | tf_op jit(solution)/shard_map/all_gather | solution.py:95
  65.6 4.1 fusion.28
  70.9 2.5 broadcast_in_dim.12
  73.4 222.6 %while.22 = (s32[]{:T(128)}, f32[3,512,768]{2,1,0:T(8,128)}, f32[8,2,256,256]{3,2,0,1:T(8,128)}, f32[256,256]{1,0:T(8,128)}, s32[3]{0:T(128)S(1)}, /*index=5*/s3...) while((s32[]{:T(128)}, f32[3,512,768]{2,1,0:T(8,128)}, ...), condition=%wide.region_5.6_spmd.clone, body=%wide.region_1.5_spmd.clone.sunk | while | flops 4323672064 | bytes 125305376 | solution.py:135
  80.6 2.6 fusion.68
  83.2 2.5 reshape.192
  85.8 6.5 copy.32
  92.3 3.2 dot_general.32
  95.4 2.3 fusion.69
  101.0 3.5 fusion.72
  106.5 8.2 copy.34
  114.8 2.6 dot_general.33
  117.4 4.9 fusion.73
  123.0 6.7 add_bitcast_fusion.3
  129.7 4.2 maximum_add_fusion.5
  135.7 9.1 dynamic_update_slice.12
  154.0 2.6 fusion.68
  156.6 2.5 reshape.192
  159.2 6.5 copy.32
  165.7 3.2 dot_general.32
  174.4 3.5 fusion.72
  179.9 8.2 copy.34
  188.2 2.6 dot_general.33
  190.8 4.9 fusion.73
  196.3 6.7 add_bitcast_fusion.3
  203.1 5.4 maximum_add_fusion.5
  210.4 9.3 dynamic_update_slice.12
  228.9 2.6 fusion.68
  231.5 2.5 reshape.192
  234.1 6.5 copy.32
  240.5 3.2 dot_general.32
  249.3 3.5 fusion.72
  254.8 8.2 copy.34
  263.1 2.6 dot_general.33
  265.7 4.9 fusion.73
  271.2 6.7 add_bitcast_fusion.3
  278.0 5.4 maximum_add_fusion.5
  285.2 8.7 dynamic_update_slice.12
  296.0 4.6 copy.21
  302.8 6.6 collective-permute-start.2
  315.9 13.1 %collective-permute-done.2 = f32[3,512,128]{2,1,0:T(8,128)} collective-permute-done((f32[3,512,128]{2,1,0:T(8,128)}, f32[3,512,128]{2,1,0:T(8,128)}, u32[]{:S(2)}, u32[]{:S(2)}) %collective-permute-start.2) | collective-permute-done | bytes 786464 | tf_op jit(solution)/shard_map/ppermute | solution.py:27
  330.5 589.2 %all-reduce.9.cloned.1.call-done = (f32[4,4,256,256]{3,2,1,0:T(8,128)}, f32[1,1,256,256]{3,2,1,0:T(8,128)}) async-done(((f32[4,4,256,256]{3,2,1,0:T(8,128)}, f32[1,1,256,256]{3,2,1,0:T(8,128)}), (f32[4,4,256,256]{3,2,1,0:T(8,128)}, f32[1,1,256,256]{3,2,1,0:T(8,128)})) %all-reduce.9.cloned.1.call-update) | async-done | bytes 4456464
  925.5 7.1 psum.7
  932.6 31.9 %all-reduce.7.cloned.1.call-done = f32[4,4,4,256]{3,2,1,0:T(4,128)} async-done(((f32[4,4,4,256]{3,2,1,0:T(4,128)}), f32[4,4,4,256]{3,2,1,0:T(4,128)}) %all-reduce.7.cloned.1.call-update) | async-done | bytes 65552
  967.3 49.7 %reduce-scatter.4.cloned.1.call-done = f32[3,128,512]{2,1,0:T(8,128)} async-done(((f32[3,512,512]{2,1,0:T(8,128)}), f32[3,128,512]{2,1,0:T(8,128)}) %reduce-scatter.4.cloned.1.call-update) | async-done | bytes 786448 | tf_op jit(solution)/shard_map/reduce_scatter | solution.py:143
  (129 shorter events, 76.5 us)
Async XLA Ops:
  7.2 27.4 %all-gather.5.cloned.1.call-start = ((), (), s32[]{:S(2)}) async-start(), calls=%async_computation.2 | async-start | bytes 1310720 | tf_op jit(solution)/shard_map/all_gather | solution.py:96
  9.0 56.6 %all-gather.3.cloned.1.call-start = ((), (), s32[]{:S(2)}) async-start(), calls=%async_computation.1 | async-start | bytes 2621440 | tf_op jit(solution)/shard_map/all_gather | solution.py:95
  11.1 908.5 %all-reduce.9.cloned.1.call-start = ((), (), s32[]{:S(2)}) async-start(), calls=%async_computation.5 | async-start | bytes 8912896
  34.5 16.9 %copy-start.8 = (bf16[2,512,512]{2,1,0:T(8,128)(2,1)S(1)}, bf16[2,512,512]{2,1,0:T(8,128)(2,1)}, u32[]{:S(2)}) copy-start(bf16[2,512,512]{2,1,0:T(8,128)(2,1)} %all-gather.5.cloned.1.call-done) | copy-start | bytes 3145732
  35.7 14.6 %collective-permute-start = (bf16[2,512,128]{2,1,0:T(8,128)(2,1)S(1)}, bf16[2,512,128]{2,1,0:T(8,128)(2,1)S(1)}, u32[]{:S(2)}, u32[]{:S(2)}) collective-permute-start(bf16[2,512,128]{2,1,0:T(8,128)(2,1)S(1)} %get-tuple-element.550), channel_id=1, source_target_pairs={{0,4},{4,8},{8,12},{12,16},{16,20},{20,24},{24,28},{28,32},{32,36}... | collective-permute-start | bytes 786440 | tf_op jit(solution)/shard_map/ppermute | solution.py:18
  39.2 12.3 %collective-permute-start.1 = (bf16[2,512,128]{2,1,0:T(8,128)(2,1)S(1)}, bf16[2,512,128]{2,1,0:T(8,128)(2,1)S(1)}, u32[]{:S(2)}, u32[]{:S(2)}) collective-permute-start(bf16[2,512,128]{2,1,0:T(8,128)(2,1)S(1)} %get-tuple-element.551), channel_id=1, source_target_pairs={{4,0},{8,4},{12,8},{16,12},{20,16},{24,20},{28,24},{32,28},{36,32}... | collective-permute-start | bytes 786440 | tf_op jit(solution)/shard_map/ppermute | solution.py:19
  65.6 4.1 copy-start.1
  70.9 2.5 copy-start.9
  70.9 2.5 copy-start.10
  79.6 1.0 copy-start.5
  97.7 2.1 copy-start
  129.7 4.2 copy-start.7
  129.7 4.3 copy-start.3
  129.7 4.3 copy-start.4
  134.0 12.8 %copy-start.2 = (bf16[8,2,256,256]{3,2,0,1:T(8,128)(2,1)S(1)}, bf16[8,2,256,256]{3,2,0,1:T(8,128)(2,1)}, u32[]{:S(2)}) copy-start(bf16[8,2,256,256]{3,2,0,1:T(8,128)(2,1)} %get-tuple-element.762) | copy-start | bytes 6291460 | tf_op jit(solution)/shard_map/while
  153.0 1.0 copy-start.5
  171.1 2.1 copy-start
  203.1 5.5 copy-start.7
  203.1 5.5 copy-start.3
  203.1 5.5 copy-start.4
  208.6 13.1 %copy-start.2 = (bf16[8,2,256,256]{3,2,0,1:T(8,128)(2,1)S(1)}, bf16[8,2,256,256]{3,2,0,1:T(8,128)(2,1)}, u32[]{:S(2)}) copy-start(bf16[8,2,256,256]{3,2,0,1:T(8,128)(2,1)} %get-tuple-element.762) | copy-start | bytes 6291460 | tf_op jit(solution)/shard_map/while
  227.9 1.0 copy-start.5
  246.0 2.1 copy-start
  278.0 5.5 copy-start.7
  278.0 5.5 copy-start.3
  278.0 5.5 copy-start.4
  283.5 12.5 %copy-start.2 = (bf16[8,2,256,256]{3,2,0,1:T(8,128)(2,1)S(1)}, bf16[8,2,256,256]{3,2,0,1:T(8,128)(2,1)}, u32[]{:S(2)}) copy-start(bf16[8,2,256,256]{3,2,0,1:T(8,128)(2,1)} %get-tuple-element.762) | copy-start | bytes 6291460 | tf_op jit(solution)/shard_map/while
  300.6 8.7 copy-start.12
  300.6 663.9 %all-reduce.7.cloned.1.call-start = ((), (), s32[]{:S(2)}) async-start(), calls=%async_computation.4 | async-start | bytes 131072
  302.8 26.2 %collective-permute-start.2 = (f32[3,512,128]{2,1,0:T(8,128)}, f32[3,512,128]{2,1,0:T(8,128)}, u32[]{:S(2)}, u32[]{:S(2)}) collective-permute-start(f32[3,512,128]{2,1,0:T(8,128)} %slice.165), channel_id=1, source_target_pairs={{4,0},{8,4},{12,8},{16,12},{20,16},{24,20},{28,24},{32,28},{36,32}... | collective-permute-start | bytes 2359304 | tf_op jit(solution)/shard_map/ppermute | solution.py:27
  314.0 607.3 %collective-permute-start.3 = (bf16[3,512,128]{2,1,0:T(8,128)(2,1)S(1)}, bf16[3,512,128]{2,1,0:T(8,128)(2,1)}, u32[]{:S(2)}, u32[]{:S(2)}) collective-permute-start(bf16[3,512,128]{2,1,0:T(8,128)(2,1)S(1)} %slice.241), channel_id=1, source_target_pairs={{0,4},{4,8},{8,12},{12,16},{16,20},{20,24},{24,28},{28,32},{32,36}... | collective-permute-start | bytes 1179656 | tf_op jit(solution)/shard_map/ppermute | solution.py:27
  921.2 2.9 copy-start.11
  921.3 95.7 %reduce-scatter.4.cloned.1.call-start = ((), (), s32[]{:S(2)}) async-start(), calls=%async_computation.3 | async-start | bytes 3932160 | tf_op jit(solution)/shard_map/reduce_scatter | solution.py:143
  922.5 1.6 copy-start.6
Sparse Core Ops, SparseCore 0:
  9.8 24.6 all-gather.4
  36.9 28.6 all-gather.2
  300.7 618.8 all-reduce.8
  922.7 41.7 all-reduce.6
  967.4 49.5 reduce-scatter.3
where the time goes:
time: 1030 us
  waiting for transfers between devices  723 us (70%)
  local copies, waits for them, and re-layouts  138 us (13%)
  other arithmetic  71.9 us (7%)
  matrix products  39.9 us (4%)
  starting transfers between devices  18.8 us (2%)
  between operations  14.6 us (1%)
  loops' own time  13.7 us (1%)
    unnamed x7, waiting for transfers between devices  621 us
    reduce_scatter x1, waiting for transfers between devices, local(): summed = lax.psum_scatter(central, 'mode', scatter_dimension=1, tiled=True)  49.7 us
    transpose x6, local copies, waits for them, and re-layouts, swap_axes(): return values.reshape(batch_count, length, 2, half_width).transpose(0, 3,...  44.1 us
    dot_general x12, matrix products, along_last(): result = jnp.dot(flattened, matrix, preferred_element_type=jnp.float32)  39.9 us
    dynamic_update_slice x3, local copies, waits for them, and re-layouts, slot_step(): lax.dynamic_update_slice(gradient, previous + term, (0, row_start, col_st...  27.1 us
    all_gather x1, waiting for transfers between devices, local(): lax.all_gather(object_half, 'mode', axis=1, tiled=True)  23.3 us
  transfers between devices with their start and end apart: 9, of which 8 were waited for; matrix products, arithmetic and copies ran while one was open for 2% of the time, Pallas kernels for 0%

commit v1 on v0

v1 whole, which is shorter than its diff:
```python
import functools

import jax
import jax.numpy as jnp
import ml_dtypes
import numpy as np
from jax import lax
from jax.experimental import pallas as pl
from jax.experimental.pallas import tpu as pltpu
from jax.sharding import PartitionSpec as P

object_reg = 0.5
probe_reg = 1.0
N = 256
bf = jnp.bfloat16
f32 = jnp.float32

def tables():
    pos = np.arange(N)
    ang = (pos[:, None] * pos[None, :] % N) * (2.0 * np.pi / N)
    sc = 1.0 / np.sqrt(float(N))
    re = (np.cos(ang) * sc).astype(ml_dtypes.bfloat16)
    im = (-np.sin(ang) * sc).astype(ml_dtypes.bfloat16)
    forward = np.block([[re, im], [-im, re]]).astype(ml_dtypes.bfloat16)
    inverse = np.block([[re, -im], [im, re]]).astype(ml_dtypes.bfloat16)
    return forward, inverse

def dot(a, b):
    return jnp.dot(a, b, preferred_element_type=f32)

def k2_kernel(rows, cols, live, ext, probe, meas, fwd, inv, grad, pg, pw,
              ext32, patch, spec, gacc, light, UN=1):
    for c in range(2):
        ext32[c, :512, :768] = ext[c].astype(f32)
        ext32[c, :512, 768:] = jnp.zeros((512, 128), f32)
        ext32[c, 512:, :] = jnp.zeros((8, 896), f32)
    gacc[...] = jnp.zeros_like(gacc)
    pg[...] = jnp.zeros_like(pg)
    pw[...] = jnp.zeros_like(pw)
    light[...] = jnp.zeros_like(light)
    def lstep(m, _):
        re = probe[m, 0].astype(f32)
        im = probe[m, 1].astype(f32)
        light[...] += re * re + im * im
        return 0
    lax.fori_loop(0, 8, lstep, 0)

    def slot(s, _):
        @pl.when(live[s] > 0)
        def _():
            row = rows[s]
            col = cols[s]
            cb = pl.multiple_of((col // 128) * 128, 128)
            cr = col - cb
            back_shift = lax.rem(384 - cr, 384)
            rb = pl.multiple_of((row // 8) * 8, 8)
            rr = row - rb
            up = lax.rem(264 - rr, 264)
            for c in range(2):
                win = ext32[c, pl.ds(rb, 264), pl.ds(cb, 384)]
                win = pltpu.roll(win, back_shift, 1)[:, :N]
                patch[c] = pltpu.roll(win, up, 0)[:N]
            pw[...] += patch[0] * patch[0] + patch[1] * patch[1]

            def first(m, power):
                pr = probe[m, 0].astype(f32)
                pi = probe[m, 1].astype(f32)
                ar = patch[0]
                ai = patch[1]
                wave = jnp.concatenate([pr * ar - pi * ai, pr * ai + pi * ar], 1).astype(bf)
                half = dot(wave, fwd[...]).astype(bf)
                stacked = jnp.concatenate([half[:, :N], half[:, N:]], 0)
                sp = dot(inv[...], stacked)
                spec[m] = sp
                return power + sp[:N] * sp[:N] + sp[N:] * sp[N:]
            power = lax.fori_loop(0, 8, first, jnp.zeros((N, N), f32), unroll=UN)
            factor = meas[s] * lax.rsqrt(jnp.maximum(power, 0.25)) - 1.0
            patch[2] = factor

            def second(m, carry):
                gr, gi = carry
                fac = patch[2]
                sp = spec[m]
                diff = jnp.concatenate([sp[:N] * fac, sp[N:] * fac], 0).astype(bf)
                bh = dot(fwd[...], diff).astype(bf)
                wide = jnp.concatenate([bh[:N], bh[N:]], 1)
                back = dot(wide, inv[...])
                br = back[:, :N]
                bi = back[:, N:]
                pr = probe[m, 0].astype(f32)
                pi = probe[m, 1].astype(f32)
                ar = patch[0]
                ai = patch[1]
                pg[m, 0] += ar * br + ai * bi
                pg[m, 1] += ar * bi - ai * br
                return gr + pr * br + pi * bi, gi + pr * bi - pi * br
            z = jnp.zeros((N, N), f32)
            gr, gi = lax.fori_loop(0, 8, second, (z, z), unroll=UN)
            pad = jnp.zeros((N, 128), f32)
            low = jnp.zeros((8, 384), f32)
            for c, term in enumerate((gr, gi, light[...])):
                moved = pltpu.roll(jnp.concatenate([term, pad], 1), cr, 1)
                moved = pltpu.roll(jnp.concatenate([moved, low], 0), rr, 0)
                gacc[c, pl.ds(rb, 264), pl.ds(cb, 384)] += moved
        return 0
    lax.fori_loop(0, 3, slot, 0)
    grad[...] = gacc[:, :512, :768]

def k2(rows, cols, live, ext, probe, meas, UN=1):
    fwd, inv = tables()
    V = pl.BlockSpec(memory_space=pltpu.VMEM)
    S = pl.BlockSpec(memory_space=pltpu.SMEM)
    return pl.pallas_call(
        functools.partial(k2_kernel, UN=UN),
        out_shape=(jax.ShapeDtypeStruct((3, 512, 768), f32),
                   jax.ShapeDtypeStruct((8, 2, N, N), f32),
                   jax.ShapeDtypeStruct((N, N), f32)),
        in_specs=[S, S, S, V, V, V, V, V],
        out_specs=(V, V, V),
        scratch_shapes=[pltpu.VMEM((2, 520, 896), f32), pltpu.VMEM((3, N, N), f32),
                        pltpu.VMEM((8, 512, N), f32), pltpu.VMEM((3, 520, 896), f32), pltpu.VMEM((N, N), f32)],
        compiler_params=pltpu.CompilerParams(vmem_limit_bytes=60 * 2**20),
        name="refine",
    )(rows, cols, live, ext, probe, meas, jnp.asarray(fwd), jnp.asarray(inv))


def extended_2(array, sides, width):
    for axis, dim in sides:
        peers, length = (lax.axis_size(axis), array.shape[dim])
        up = [(i, (i + 1) % peers) for i in range(peers - 1)]
        down = [(j, i) for i, j in up]
        last = lax.slice_in_dim(array, length - width, length, axis=dim)
        leading = lax.slice_in_dim(array, 0, width, axis=dim)
        before = lax.ppermute(last, axis, up)
        after = lax.ppermute(leading, axis, down)
        array = jnp.concatenate([before, array, after], axis=dim)
    return array


def passed_along(block, axis, distance):
    devices = range(lax.axis_size(axis))
    route = [(i - distance, i) for i in devices if i - distance in devices]
    return lax.ppermute(block, axis, route)


def local(object_field, probe, measured, scan_rows, scan_cols, counts):
    modes_here = probe.shape[0]
    length = probe.shape[2]
    margin = length // 2
    tile_width = object_field.shape[2]
    groups = lax.axis_size("mode")
    tiles = lax.axis_size("tile")
    slots = scan_rows.shape[0]
    probe_half = probe.astype(jnp.bfloat16)
    object_half = object_field.astype(jnp.bfloat16)
    probe_all, object_rows = (
        lax.all_gather(probe_half, "mode", axis=0, tiled=True),
        lax.all_gather(object_half, "mode", axis=1, tiled=True),
    )
    extended = extended_2(object_rows, (("tile", 2),), margin)
    first_slot = lax.axis_index("mode") * slots
    live = (first_slot + jnp.arange(slots, dtype=jnp.int32) < counts[0]).astype(jnp.int32)
    gradient, probe_grad, weight_sum = k2(
        scan_rows, scan_cols, live, extended, probe_all, measured, UN=2
    )
    left_rim = gradient[:, :, :margin]
    right_rim = gradient[:, :, tile_width + margin :]
    central = gradient[:, :, margin : tile_width + margin]
    from_right = passed_along(left_rim, "tile", -1)
    from_left = passed_along(right_rim.astype(jnp.bfloat16), "tile", 1).astype(right_rim.dtype)
    central = central.at[:, :, tile_width - margin :].add(from_right)
    central = central.at[:, :, :margin].add(from_left)
    summed = lax.psum_scatter(central, "mode", scatter_dimension=1, tiled=True)
    object_out = object_field + summed[:2] / (summed[2] + object_reg)
    grouped = probe_grad.reshape(groups, 2 * modes_here, length, length)
    power_plane = weight_sum.reshape(1, 1, length, length)
    by_mode = lax.psum_scatter(grouped, "mode", scatter_dimension=0, tiled=True)
    owned = lax.psum_scatter(by_mode, "tile", scatter_dimension=2, tiled=True)
    power_band = lax.psum_scatter(power_plane, "tile", scatter_dimension=2, tiled=True)
    power_total = lax.psum(power_band, "mode")
    band_rows = length // tiles
    first_row = lax.axis_index("tile") * band_rows
    probe_rows = lax.dynamic_slice_in_dim(probe, first_row, band_rows, 2)
    steps_term = owned[0].reshape(modes_here, 2, band_rows, length)
    probe_out = probe_rows + steps_term / (power_total[0, 0] + probe_reg)
    return (object_out, probe_out)


def solution(mesh):
    return jax.shard_map(
        local,
        mesh=mesh,
        in_specs=(
            P(None, "mode", "tile"),
            P("mode", None, None, None),
            P(("tile", "mode"), None, None),
            P(("tile", "mode")),
            P(("tile", "mode")),
            P("tile"),
        ),
        out_specs=(P(None, "mode", "tile"), P("mode", None, "tile", None)),
        check_vma=False,
    )
```

time: 1030 us -> 827 us (0.80)
  local copies, waits for them, and re-layouts: 138 us -> 9.33 us
  other arithmetic: 71.9 us -> 12.8 us
  matrix products: 39.9 us -> 0 us
  waiting for transfers between devices: 723 us -> 755 us
  loops' own time: 13.7 us -> 0 us
    reduce_scatter x0 -> x1, waiting for transfers between devices: none -> 60.2 us  [local(): by_mode = lax.psum_scatter(grouped, 'mode', scatter_dimension=0, tiled=True)]
    transpose x6 -> x0, local copies, waits for them, and re-layouts: 44.1 us -> none  [swap_axes(): return values.reshape(batch_count, length, 2, half_width).transpose(0, 3,...]
    dot_general x12 -> x0, matrix products: 39.9 us -> none  [along_last(): result = jnp.dot(flattened, matrix, preferred_element_type=jnp.float32)]
    unnamed x7 -> x6, waiting for transfers between devices: 621 us -> 593 us
    dynamic_update_slice x3 -> x0, local copies, waits for them, and re-layouts: 27.1 us -> none  [slot_step(): lax.dynamic_update_slice(gradient, previous + term, (0, row_start, col_st...]
    add x9 -> x0, other arithmetic: 26.3 us -> none  [the longest x3 15.1 us: slot_step(): probe_grad = probe_grad + jnp.stack([term_re, term_im], 1)]
    another operation x6 -> x0, other arithmetic: 22.4 us -> none  [the longest x3 20.2 us: slot_step(): probe_grad = probe_grad + jnp.stack([term_re, term_im], 1)]
    dot_general x6 -> x0, local copies, waits for them, and re-layouts: 17.3 us -> none  [along_last(): result = jnp.dot(flattened, matrix, preferred_element_type=jnp.float32)]
where the time goes in v1:
time: 827 us; the launch traced here: 826 us
  waiting for transfers between devices  755 us (91%)
  starting transfers between devices  19 us (2%)
  between operations  15.2 us (2%)
  other arithmetic  12.8 us (2%)
  local copies, waits for them, and re-layouts  9.33 us (1%)
    unnamed x6, waiting for transfers between devices  593 us
    reduce_scatter x1, waiting for transfers between devices, local(): by_mode = lax.psum_scatter(grouped, 'mode', scatter_dimension=0, tiled=True)  60.2 us
    reduce_scatter x1, waiting for transfers between devices, local(): summed = lax.psum_scatter(central, 'mode', scatter_dimension=1, tiled=True)  51.1 us
    all_gather x1, waiting for transfers between devices, local(): lax.all_gather(object_half, 'mode', axis=1, tiled=True)  23.3 us
  transfers between devices with their start and end apart: 9, of which 8 were waited for; matrix products, arithmetic and copies ran while one was open for 2% of the time, Pallas kernels for 0%

profile of v1, /device:TPU:6, one launch (start us, length us, event | category | flops | bytes accessed | tf_op | source)
XLA Modules:
  0.0 826.2 jit_solution(16130314406164493234)
XLA Ops:
  7.2 0.0 all-gather.3.cloned.1.call-start
  7.2 1.8 convert_element_type.14
  9.0 0.0 all-gather.3.cloned.1.call-update
  9.0 0.0 all-gather.5.cloned.1.call-start
  9.1 2.1 convert_element_type.15
  11.1 0.0 all-gather.5.cloned.1.call-update
  11.2 0.0 reduce-scatter.7.cloned.1.call-start
  11.2 23.3 %all-gather.3.cloned.1.call-done = bf16[2,512,512]{2,1,0:T(8,128)(2,1)} async-done(((bf16[2,128,512]{2,1,0:T(8,128)(2,1)}), bf16[2,512,512]{2,1,0:T(8,128)(2,1)}) %all-gather.3.cloned.1.call-update) | async-done | bytes 1048592 | tf_op jit(solution)/shard_map/all_gather | solution.py:158
  34.5 1.1 fusion.3
  35.6 3.5 collective-permute-start
  39.1 6.6 collective-permute-start.1
  46.3 0.5 compare_convert_fusion.live
  46.8 3.3 collective-permute-done
  50.2 1.2 collective-permute-done.1
  51.3 2.6 pad_maximum_fusion.ext
  53.9 11.7 %all-gather.5.cloned.1.call-done.probe = bf16[8,2,256,256]{3,2,1,0:T(8,128)(2,1)} async-done(((bf16[2,2,256,256]{3,2,1,0:T(8,128)(2,1)}), bf16[8,2,256,256]{3,2,1,0:T(8,128)(2,1)}) %all-gather.5.cloned.1.call-update) | async-done | bytes 2097168 | tf_op jit(solution)/shard_map/all_gather | solution.py:157
  65.6 7.4 refine.1
  73.0 0.0 reduce-scatter.7.cloned.1.call-update
  73.1 0.0 reduce-scatter.5.cloned.1.call-start
  73.1 1.2 slice.75
  74.3 6.8 collective-permute-start.2
  81.1 1.2 slice.97
  82.3 1.9 collective-permute-start.3
  84.2 2.2 slice.73
  86.4 11.9 %collective-permute-done.2 = f32[3,512,128]{2,1,0:T(8,128)S(1)} collective-permute-done((f32[3,512,128]{2,1,0:T(8,128)S(1)}, f32[3,512,128]{2,1,0:T(8,128)S(1)}, u32[]{:S(2)}, u32[]{:S(2)}) %collective-permute-start.2) | collective-permute-done | bytes 786464 | tf_op jit(solution)/shard_map/ppermute | solution.py:143
  98.3 1.3 add_dynamic-update-slice_fusion
  99.5 0.0 copy-start.1
  99.6 0.0 collective-permute-done.3
  99.6 0.2 fusion
  99.7 0.0 copy-start
  99.8 1.6 copy-done
  101.4 0.0 reduce-scatter.5.cloned.1.call-update
  101.4 0.0 all-reduce.5.cloned.1.call-start
  101.5 60.2 %reduce-scatter.7.cloned.1.call-done = f32[1,4,256,256]{3,2,1,0:T(8,128)} async-done(((f32[4,4,256,256]{3,2,1,0:T(8,128)}), f32[1,4,256,256]{3,2,1,0:T(8,128)}) %reduce-scatter.7.cloned.1.call-update) | async-done | bytes 1048592 | tf_op jit(solution)/shard_map/reduce_scatter | solution.py:177
  161.7 0.0 all-reduce.5.cloned.1.call-update
  161.7 0.0 copy-done.1
  161.7 0.6 dynamic-slice.16
  162.9 51.1 %reduce-scatter.5.cloned.1.call-done = f32[3,128,512]{2,1,0:T(8,128)} async-done(((f32[3,512,512]{2,1,0:T(8,128)}), f32[3,128,512]{2,1,0:T(8,128)}) %reduce-scatter.5.cloned.1.call-update) | async-done | bytes 786448 | tf_op jit(solution)/shard_map/reduce_scatter | solution.py:173
  214.0 1.0 fusion.2
  215.0 2.1 fusion.1
  217.1 592.6 %all-reduce.5.cloned.1.call-done = (f32[1,4,256,256]{3,2,1,0:T(8,128)}, f32[1,1,256,256]{3,2,1,0:T(8,128)}) async-done(((f32[1,4,256,256]{3,2,1,0:T(8,128)}, f32[1,1,256,256]{3,2,1,0:T(8,128)}), (f32[1,4,256,256]{3,2,1,0:T(8,128)}, f32[1,1,256,256]{3,2,1,0:T(8,128)})) %all-reduce.5.cloned.1.call-update) | async-done | bytes 1310736
  809.7 0.8 constant_dynamic-slice_fusion.1
  810.4 0.7 constant_dynamic-slice_fusion
  811.1 7.1 psum.7
  818.3 1.4 divide_add_fusion
  (1 shorter events, 0.0 us)
Async XLA Ops:
  7.2 27.4 %all-gather.3.cloned.1.call-start = ((), (), s32[]{:S(2)}) async-start(), calls=%async_computation.2 | async-start | bytes 1310720 | tf_op jit(solution)/shard_map/all_gather | solution.py:158
  9.0 56.6 %all-gather.5.cloned.1.call-start = ((), (), s32[]{:S(2)}) async-start(), calls=%async_computation.3 | async-start | bytes 2621440 | tf_op jit(solution)/shard_map/all_gather | solution.py:157
  11.2 150.5 %reduce-scatter.7.cloned.1.call-start = ((), (), s32[]{:S(2)}) async-start(), calls=%async_computation.5 | async-start | bytes 5242880 | tf_op jit(solution)/shard_map/reduce_scatter | solution.py:177
  35.6 14.6 %collective-permute-start = (bf16[2,512,128]{2,1,0:T(8,128)(2,1)S(1)}, bf16[2,512,128]{2,1,0:T(8,128)(2,1)S(1)}, u32[]{:S(2)}, u32[]{:S(2)}) collective-permute-start(bf16[2,512,128]{2,1,0:T(8,128)(2,1)S(1)} %get-tuple-element.34), channel_id=1, source_target_pairs={{0,4},{4,8},{8,12},{12,16},{16,20},{20,24},{24,28},{28,32},{32,36}... | collective-permute-start | bytes 786440 | tf_op jit(solution)/shard_map/ppermute | solution.py:134
  39.1 12.3 %collective-permute-start.1 = (bf16[2,512,128]{2,1,0:T(8,128)(2,1)S(1)}, bf16[2,512,128]{2,1,0:T(8,128)(2,1)S(1)}, u32[]{:S(2)}, u32[]{:S(2)}) collective-permute-start(bf16[2,512,128]{2,1,0:T(8,128)(2,1)S(1)} %get-tuple-element.35), channel_id=1, source_target_pairs={{4,0},{8,4},{12,8},{16,12},{20,16},{24,20},{28,24},{32,28},{36,32}... | collective-permute-start | bytes 786440 | tf_op jit(solution)/shard_map/ppermute | solution.py:135
  73.1 141.0 %reduce-scatter.5.cloned.1.call-start = ((), (), s32[]{:S(2)}) async-start(), calls=%async_computation.4 | async-start | bytes 3932160 | tf_op jit(solution)/shard_map/reduce_scatter | solution.py:173
  74.3 24.0 %collective-permute-start.2 = (f32[3,512,128]{2,1,0:T(8,128)S(1)}, f32[3,512,128]{2,1,0:T(8,128)S(1)}, u32[]{:S(2)}, u32[]{:S(2)}) collective-permute-start(f32[3,512,128]{2,1,0:T(8,128)S(1)} %slice.75), channel_id=1, source_target_pairs={{4,0},{8,4},{12,8},{16,12},{20,16},{24,20},{28,24},{32,28},{36,32}... | collective-permute-start | bytes 2359304 | tf_op jit(solution)/shard_map/ppermute | solution.py:143
  82.3 17.3 %collective-permute-start.3 = (bf16[3,512,128]{2,1,0:T(8,128)(2,1)S(1)}, bf16[3,512,128]{2,1,0:T(8,128)(2,1)S(1)}, u32[]{:S(2)}, u32[]{:S(2)}) collective-permute-start(bf16[3,512,128]{2,1,0:T(8,128)(2,1)S(1)} %slice.97), channel_id=1, source_target_pairs={{0,4},{4,8},{8,12},{12,16},{16,20},{20,24},{24,28},{28,32},{32,36}... | collective-permute-start | bytes 1179656 | tf_op jit(solution)/shard_map/ppermute | solution.py:143
  99.5 62.1 %copy-start.1 = (u32[256]{0:T(256)S(1)}, u32[256]{0:T(256)}, u32[]{:S(2)}) copy-start(u32[256]{0:T(256)} %constant.88) | copy-start | bytes 3076
  99.7 1.6 copy-start
  101.4 708.3 %all-reduce.5.cloned.1.call-start = ((), (), s32[]{:S(2)}) async-start(), calls=%async_computation.6 | async-start | bytes 2621440
Sparse Core Ops, SparseCore 0:
  9.8 24.6 all-gather.2
  36.9 28.6 all-gather.4
  73.2 88.4 reduce-scatter.6
  164.5 49.4 reduce-scatter.4
  216.6 593.0 all-reduce.4

commit v2 on v1

--- a/solution.py
+++ b/solution.py
@@ -12,8 +12,12 @@
 object_reg = 0.5
 probe_reg = 1.0
 N = 256
+X, Y, Z = 4, 4, 8
 bf = jnp.bfloat16
 f32 = jnp.float32
+MESH = pl.DeviceIdType.MESH
+XY = [(i, j) for i in range(X) for j in range(Y) if i or j]
+
 
 def tables():
     pos = np.arange(N)
@@ -25,11 +29,158 @@
     inverse = np.block([[re, -im], [im, re]]).astype(ml_dtypes.bfloat16)
     return forward, inverse
 
+
 def dot(a, b):
     return jnp.dot(a, b, preferred_element_type=f32)
 
-def k2_kernel(rows, cols, live, ext, probe, meas, fwd, inv, grad, pg, pw,
-              ext32, patch, spec, gacc, light, UN=1):
+
+def here():
+    tile = lax.axis_index("tile")
+    group = lax.axis_index("mode")
+    x = (group // 2) * 2 + tile // (Y * Z)
+    return tile, group, x, (tile // Z) % Y, tile % Z, group % 2
+
+
+def device(x, y, z, core):
+    return {"tile": (x % 2) * (Y * Z) + y * Z + z, "mode": (x // 2) * 2 + core}
+
+
+def greet(partners):
+    barrier = pltpu.get_barrier_semaphore()
+    for partner in partners:
+        pl.semaphore_signal(barrier, inc=1, device_id=partner, device_id_type=MESH)
+    pl.semaphore_wait(barrier, len(partners))
+
+
+def sender(send_sem, recv_sem):
+    def make(index, src, dst, target):
+        return pltpu.make_async_remote_copy(
+            src_ref=src, dst_ref=dst, send_sem=send_sem.at[index], recv_sem=recv_sem.at[index],
+            device_id=target, device_id_type=MESH,
+        )
+    return make
+
+
+def gather_kernel(obj, probe, ext, modes, block, send_sem, recv_sem):
+    tile, group, x, y, z, core = here()
+    tiles = X * Y * Z // 2
+    sibling = device(x, y, z, 1 - core)
+    opposite = device((x + 2) % X, y, z, core)
+    across = device(X - 1 - x, y, z, core)
+    along_y = [device(x, (y + i) % Y, z, core) for i in (1, 3, 2)]
+    before, after = (tile + tiles - 1) % tiles, (tile + 1) % tiles
+    other = (group + 2) % 4
+    halo_to = [
+        {"tile": before, "mode": group}, {"tile": before, "mode": other},
+        {"tile": after, "mode": group}, {"tile": after, "mode": other},
+    ]
+    block[...] = obj[...].astype(bf)
+    for k in range(2):
+        for c in range(2):
+            modes[group, 2 * k + c] = probe[k, c].astype(bf)
+    mine = pl.multiple_of(group * 128, 128)
+    theirs = pl.multiple_of(other * 128, 128)
+    ext[:, pl.ds(mine, 128), 128:640] = block[...]
+
+    @pl.when(tile == 0)
+    def _():
+        ext[:, :, :128] = jnp.zeros((2, 512, 128), bf)
+
+    @pl.when(tile == tiles - 1)
+    def _():
+        ext[:, :, 640:] = jnp.zeros((2, 512, 128), bf)
+
+    greet([sibling, opposite, across] + along_y + halo_to)
+    make = sender(send_sem, recv_sem)
+
+    def rows(start, low, width):
+        return ext.at[:, pl.ds(start, 128), pl.ds(low, width)]
+
+    def plane(which, index):
+        return modes.at[which, pl.ds(index, 1)]
+
+    far = make(0, block, rows(mine, 128, 512), opposite)
+    far.start()
+    cut = make(1, plane(group, y), plane(group, y), across)
+    cut.start()
+    left, right = block.at[:, :, pl.ds(0, 128)], block.at[:, :, pl.ds(384, 128)]
+    halo = [
+        make(2, left, rows(mine, 640, 128), halo_to[0]),
+        make(3, left, rows(mine, 640, 128), halo_to[1]),
+        make(4, right, rows(mine, 0, 128), halo_to[2]),
+        make(5, right, rows(mine, 0, 128), halo_to[3]),
+    ]
+    sends = (tile > 0, tile > 0, tile < tiles - 1, tile < tiles - 1)
+    gets = (tile < tiles - 1, tile < tiles - 1, tile > 0, tile > 0)
+    for flag, copy in zip(sends, halo):
+        pl.when(flag)(copy.start)
+    near = make(6, block, rows(mine, 128, 512), sibling)
+    near.start()
+    own = make(7, modes.at[group], modes.at[group], sibling)
+    own.start()
+
+    passed = []
+
+    def pass_on(index, ref):
+        copy = make(index, ref, ref, sibling)
+        copy.start()
+        passed.append(copy)
+
+    cut.wait_recv()
+    spread = []
+    for i, target in enumerate(along_y):
+        copy = make(8 + i, plane(other, y), plane(other, y), target)
+        copy.start()
+        spread.append(copy)
+    pass_on(11, plane(other, y))
+    halo_kept = []
+    for i, (flag, start, low) in enumerate(
+        zip(gets, (mine, theirs, mine, theirs), (640, 640, 0, 0))
+    ):
+        on = make(12 + i, rows(start, low, 128), rows(start, low, 128), sibling)
+        halo_kept.append((flag, on))
+
+        @pl.when(flag)
+        def _():
+            halo[i].wait_recv()
+            on.start()
+    far.wait_recv()
+    pass_on(16, rows(theirs, 128, 512))
+    for i, step in enumerate((1, 3, 2)):
+        spread[i].wait_recv()
+        pass_on(17 + i, plane(other, (y + Y - step) % Y))
+    for copy in [near, own] + passed:
+        copy.wait()
+    for copy in [far, cut] + spread:
+        copy.wait_send()
+    for flag, copy in zip(sends, halo):
+        pl.when(flag)(copy.wait_send)
+    for flag, copy in halo_kept:
+        pl.when(flag)(copy.wait)
+
+
+def gather(obj, probe):
+    whole = pl.BlockSpec(memory_space=pltpu.VMEM)
+    return pl.pallas_call(
+        gather_kernel,
+        out_shape=(
+            jax.ShapeDtypeStruct((2, 512, 768), bf), jax.ShapeDtypeStruct((4, 4, N, N), bf)
+        ),
+        in_specs=[whole, whole],
+        out_specs=(whole, whole),
+        scratch_shapes=[
+            pltpu.VMEM((2, 128, 512), bf),
+            pltpu.SemaphoreType.DMA((20,)), pltpu.SemaphoreType.DMA((20,)),
+        ],
+        compiler_params=pltpu.CompilerParams(
+            collective_id=0, has_side_effects=True, vmem_limit_bytes=40 * 2**20
+        ),
+        name="gather",
+    )(obj, probe)
+
+
+def k2_kernel(rows, cols, live, ext, probe, meas, fwd, inv, grad, pg_out, pw,
+              pg, ext32, patch, spec, gacc, light, UN=1):
     for c in range(2):
         ext32[c, :512, :768] = ext[c].astype(f32)
         ext32[c, :512, 768:] = jnp.zeros((512, 128), f32)
@@ -105,85 +256,179 @@
         return 0
     lax.fori_loop(0, 3, slot, 0)
     grad[...] = gacc[:, :512, :768]
+    pg_out[...] = pg[...].astype(bf)
 
 def k2(rows, cols, live, ext, probe, meas, UN=1):
     fwd, inv = tables()
+    probe = probe.reshape(8, 2, N, N)
     V = pl.BlockSpec(memory_space=pltpu.VMEM)
     S = pl.BlockSpec(memory_space=pltpu.SMEM)
     return pl.pallas_call(
         functools.partial(k2_kernel, UN=UN),
         out_shape=(jax.ShapeDtypeStruct((3, 512, 768), f32),
-                   jax.ShapeDtypeStruct((8, 2, N, N), f32),
+                   jax.ShapeDtypeStruct((8, 2, N, N), bf),
                    jax.ShapeDtypeStruct((N, N), f32)),
         in_specs=[S, S, S, V, V, V, V, V],
         out_specs=(V, V, V),
-        scratch_shapes=[pltpu.VMEM((2, 520, 896), f32), pltpu.VMEM((3, N, N), f32),
+        scratch_shapes=[pltpu.VMEM((8, 2, N, N), f32), pltpu.VMEM((2, 520, 896), f32), pltpu.VMEM((3, N, N), f32),
                         pltpu.VMEM((8, 512, N), f32), pltpu.VMEM((3, 520, 896), f32), pltpu.VMEM((N, N), f32)],
         compiler_params=pltpu.CompilerParams(vmem_limit_bytes=60 * 2**20),
         name="refine",
     )(rows, cols, live, ext, probe, meas, jnp.asarray(fwd), jnp.asarray(inv))
 
 
-def extended_2(array, sides, width):
-    for axis, dim in sides:
-        peers, length = (lax.axis_size(axis), array.shape[dim])
-        up = [(i, (i + 1) % peers) for i in range(peers - 1)]
-        down = [(j, i) for i, j in up]
-        last = lax.slice_in_dim(array, length - width, length, axis=dim)
-        leading = lax.slice_in_dim(array, 0, width, axis=dim)
-        before = lax.ppermute(last, axis, up)
-        after = lax.ppermute(leading, axis, down)
-        array = jnp.concatenate([before, array, after], axis=dim)
-    return array
-
-
-def passed_along(block, axis, distance):
-    devices = range(lax.axis_size(axis))
-    route = [(i - distance, i) for i in devices if i - distance in devices]
-    return lax.ppermute(block, axis, route)
+def spread_kernel(grad, probe_sum, power, obj, probe_rows, object_out, probe_out,
+                  sent_power, got_obj, got_probe, got_power, out_obj, out_halo, got_center, got_halo,
+                  pieces, got_piece, bands, got_band, send_sem, recv_sem):
+    tile, group, x, y, z, core = here()
+    tiles = X * Y * Z // 2
+    x_hi = group // 2
+    sibling = device(x, y, z, 1 - core)
+    opposite = device((x + 2) % X, y, z, core)
+    before, after = (tile + tiles - 1) % tiles, (tile + 1) % tiles
+    other = (group + 2) % 4
+    halo_to = [
+        {"tile": before, "mode": group}, {"tile": before, "mode": other},
+        {"tile": after, "mode": group}, {"tile": after, "mode": other},
+    ]
+    in_plane = [device((x + i) % X, (y + j) % Y, z, core) for i, j in XY]
+    along_z = [device(x, y, (z + i) % Z, core) for i in range(1, Z)]
+    make = sender(send_sem, recv_sem)
+
+    sent_power[...] = power[...].astype(bf)
+    greet([sibling] + halo_to + in_plane + along_z)
+
+    first = []
+    for h in range(2):
+        start = pl.multiple_of((2 * h + 1 - core) * 128, 128)
+        first.append(make(h, probe_sum.at[2 * h + 1 - core], got_probe.at[h], sibling))
+        first.append(make(2 + h, grad.at[:, pl.ds(start, 128), :], got_obj.at[h], sibling))
+    first.append(make(4, sent_power, got_power, sibling))
+    for copy in first:
+        copy.start()
+    for i in (0, 2, 4):
+        first[i].wait_recv()
+    total_power = (sent_power[...].astype(f32) + got_power[...].astype(f32)).astype(bf)
+    for h in range(2):
+        pieces[h, 4] = total_power
+        for k in range(4):
+            pieces[h, k] = (
+                probe_sum[2 * h + core, k].astype(f32) + got_probe[h, k].astype(f32)
+            ).astype(bf)
+
+    def band(px, py):
+        start = pl.multiple_of((px % 2) * 128 + py * 32, 32)
+        return pieces.at[px // 2, :, pl.ds(start, 32), :]
+
+    second = []
+    for k, (i, j) in enumerate(XY):
+        copy = make(5 + k, band((x + i) % X, (y + j) % Y), got_piece.at[k], in_plane[k])
+        copy.start()
+        second.append(copy)
+
+    first[1].wait_recv()
+    first[3].wait_recv()
+    mine = pl.multiple_of(group * 128, 128)
+    theirs = pl.multiple_of(other * 128, 128)
+    for k in range(3):
+        out_obj[k] = (grad[k, pl.ds(theirs, 128), :] + got_obj[1 - x_hi, k]).astype(bf)
+        out_halo[0, k] = (grad[k, pl.ds(mine, 128), :128] + got_obj[x_hi, k, :, :128]).astype(bf)
+        out_halo[1, k] = (grad[k, pl.ds(mine, 128), 640:] + got_obj[x_hi, k, :, 640:]).astype(bf)
+    third = [
+        make(20, out_obj.at[:, :, pl.ds(128, 512)], got_center, opposite),
+        make(21, out_halo.at[0], got_halo.at[0], halo_to[0]),
+        make(22, out_obj.at[:, :, pl.ds(0, 128)], got_halo.at[1], halo_to[1]),
+        make(23, out_halo.at[1], got_halo.at[2], halo_to[2]),
+        make(24, out_obj.at[:, :, pl.ds(640, 128)], got_halo.at[3], halo_to[3]),
+    ]
+    for copy in third:
+        copy.start()
+
+    start = pl.multiple_of((x % 2) * 128 + y * 32, 32)
+    total = pieces[x_hi, :, pl.ds(start, 32), :].astype(f32)
+    for k in range(len(XY)):
+        second[k].wait_recv()
+        total = total + got_piece[k].astype(f32)
+    for part in range(Z):
+        for k in range(5):
+            bands[part, 4 * k:4 * k + 4] = total[k, 4 * part:4 * part + 4]
+    fourth = []
+    for i in range(1, Z):
+        copy = make(24 + i, bands.at[(z + i) % Z], got_band.at[i - 1], along_z[i - 1])
+        copy.start()
+        fourth.append(copy)
+
+    for copy in third:
+        copy.wait_recv()
+    keep_left = jnp.where(tile > 0, 1.0, 0.0)
+    keep_right = jnp.where(tile < tiles - 1, 1.0, 0.0)
+    parts = []
+    for k in range(3):
+        center = grad[k, pl.ds(mine, 128), 128:640] + got_obj[x_hi, k, :, 128:640]
+        center = center + got_center[k].astype(f32)
+        from_right = (got_halo[0, k].astype(f32) + got_halo[1, k].astype(f32)) * keep_right
+        from_left = (got_halo[2, k].astype(f32) + got_halo[3, k].astype(f32)) * keep_left
+        parts.append(jnp.concatenate(
+            [center[:, :128] + from_left, center[:, 128:384], center[:, 384:] + from_right], 1
+        ))
+    for k in range(2):
+        object_out[k] = obj[k] + parts[k] / (parts[2] + object_reg)
+
+    final = bands[z]
+    for i in range(Z - 1):
+        fourth[i].wait_recv()
+        final = final + got_band[i]
+    weight = final[16:20] + probe_reg
+    for k in range(4):
+        probe_out[k] = probe_rows[k] + final[4 * k:4 * k + 4] / weight
+    for copy in first + second + third + fourth:
+        copy.wait_send()
+
+
+def spread(grad, probe_sum, power, obj, probe_rows):
+    whole = pl.BlockSpec(memory_space=pltpu.VMEM)
+    return pl.pallas_call(
+        spread_kernel,
+        out_shape=(
+            jax.ShapeDtypeStruct((2, 128, 512), f32), jax.ShapeDtypeStruct((4, 4, N), f32)
+        ),
+        in_specs=[whole] * 5,
+        out_specs=(whole, whole),
+        scratch_shapes=[
+            pltpu.VMEM((N, N), bf),
+            pltpu.VMEM((2, 3, 128, 768), f32),
+            pltpu.VMEM((2, 4, N, N), bf),
+            pltpu.VMEM((N, N), bf),
+            pltpu.VMEM((3, 128, 768), bf),
+            pltpu.VMEM((2, 3, 128, 128), bf),
+            pltpu.VMEM((3, 128, 512), bf),
+            pltpu.VMEM((4, 3, 128, 128), bf),
+            pltpu.VMEM((2, 5, N, N), bf),
+            pltpu.VMEM((len(XY), 5, 32, N), bf),
+            pltpu.VMEM((Z, 24, N), f32),
+            pltpu.VMEM((Z - 1, 24, N), f32),
+            pltpu.SemaphoreType.DMA((32,)), pltpu.SemaphoreType.DMA((32,)),
+        ],
+        compiler_params=pltpu.CompilerParams(
+            collective_id=1, has_side_effects=True, vmem_limit_bytes=50 * 2**20
+        ),
+        name="spread",
+    )(grad, probe_sum, power, obj, probe_rows)
 
 
 def local(object_field, probe, measured, scan_rows, scan_cols, counts):
-    modes_here = probe.shape[0]
-    length = probe.shape[2]
-    margin = length // 2
-    tile_width = object_field.shape[2]
-    groups = lax.axis_size("mode")
-    tiles = lax.axis_size("tile")
     slots = scan_rows.shape[0]
-    probe_half = probe.astype(jnp.bfloat16)
-    object_half = object_field.astype(jnp.bfloat16)
-    probe_all, object_rows = (
-        lax.all_gather(probe_half, "mode", axis=0, tiled=True),
-        lax.all_gather(object_half, "mode", axis=1, tiled=True),
-    )
-    extended = extended_2(object_rows, (("tile", 2),), margin)
     first_slot = lax.axis_index("mode") * slots
     live = (first_slot + jnp.arange(slots, dtype=jnp.int32) < counts[0]).astype(jnp.int32)
-    gradient, probe_grad, weight_sum = k2(
+    extended, probe_all = gather(object_field, probe)
+    gradient, probe_sum, power = k2(
         scan_rows, scan_cols, live, extended, probe_all, measured, UN=2
     )
-    left_rim = gradient[:, :, :margin]
-    right_rim = gradient[:, :, tile_width + margin :]
-    central = gradient[:, :, margin : tile_width + margin]
-    from_right = passed_along(left_rim, "tile", -1)
-    from_left = passed_along(right_rim.astype(jnp.bfloat16), "tile", 1).astype(right_rim.dtype)
-    central = central.at[:, :, tile_width - margin :].add(from_right)
-    central = central.at[:, :, :margin].add(from_left)
-    summed = lax.psum_scatter(central, "mode", scatter_dimension=1, tiled=True)
-    object_out = object_field + summed[:2] / (summed[2] + object_reg)
-    grouped = probe_grad.reshape(groups, 2 * modes_here, length, length)
-    power_plane = weight_sum.reshape(1, 1, length, length)
-    by_mode = lax.psum_scatter(grouped, "mode", scatter_dimension=0, tiled=True)
-    owned = lax.psum_scatter(by_mode, "tile", scatter_dimension=2, tiled=True)
-    power_band = lax.psum_scatter(power_plane, "tile", scatter_dimension=2, tiled=True)
-    power_total = lax.psum(power_band, "mode")
-    band_rows = length // tiles
-    first_row = lax.axis_index("tile") * band_rows
-    probe_rows = lax.dynamic_slice_in_dim(probe, first_row, band_rows, 2)
-    steps_term = owned[0].reshape(modes_here, 2, band_rows, length)
-    probe_out = probe_rows + steps_term / (power_total[0, 0] + probe_reg)
-    return (object_out, probe_out)
+    probe_rows = lax.dynamic_slice_in_dim(probe, lax.axis_index("tile") * 4, 4, 2)
+    object_out, probe_out = spread(
+        gradient, probe_sum.reshape(4, 4, N, N), power, object_field, probe_rows.reshape(4, 4, N)
+    )
+    return object_out, probe_out.reshape(2, 2, 4, N)
 
 
 def solution(mesh):

time: 827 us -> 131 us (0.16)
  the two profiles are of different devices: /device:TPU:6 before, /device:TPU:16 now
where the time goes in v2:
time: 131 us
  Pallas kernels  119 us (91%)
  local copies, waits for them, and re-layouts  9.49 us (7%)
  between operations  1.32 us (1%)
    pallas_call x1, Pallas kernels, spread(): pl.pallas_call(spread_kernel, out_shape=(jax.ShapeDtypeStruct((2, 128, 51...  61.4 us
    pallas_call x1, Pallas kernels, gather(): pl.pallas_call(gather_kernel, out_shape=(jax.ShapeDtypeStruct((2, 512, 76...  29.3 us
    pallas_call x1, Pallas kernels, k2(): pl.pallas_call(functools.partial(k2_kernel, UN=UN), out_shape=(jax.ShapeD...  28.5 us
    unnamed x16, local copies, waits for them, and re-layouts  8.73 us

profile of v2, /device:TPU:16, one launch (start us, length us, event | category | flops | bytes accessed | tf_op | source)
XLA Modules:
  0.0 130.5 jit_solution(12402382098648178104)
XLA Ops:
  1.3 0.5 compare_convert_fusion.live
  1.8 0.0 copy-start.2
  1.8 1.0 copy-done.2
  2.8 0.0 copy-start.5
  2.8 1.2 copy-done.5
  4.0 29.3 %gather.1 = (bf16[2,512,768]{2,1,0:T(8,128)(2,1)S(1)}, bf16[4,4,256,256]{3,2,1,0:T(8,128)(2,1)S(1)}) custom-call(f32[2,128,512]{2,1,0:T(8,128)S(1)} %copy-done.2, f32[2,2,256,256]{3,2,1,0:T(8,128)S(1)} %copy-done.5), custom_call_target="tpu_custom_call" | custom-call | tf_op jit(solution)/shard_map/gather/pallas_call | solution.py:164
  33.3 0.0 copy-start
  33.3 1.4 %copy-done = bf16[4,4,256,256]{3,2,1,0:T(8,128)(2,1)} copy-done((bf16[4,4,256,256]{3,2,1,0:T(8,128)(2,1)}, bf16[4,4,256,256]{3,2,1,0:T(8,128)(2,1)S(1)}, u32[]{:S(2)}) %copy-start) | copy-done | bytes 2097176
  34.7 0.0 copy-start.4
  34.7 1.2 copy-done.4
  35.9 0.0 copy-start.3
  35.9 28.5 %refine.1 = (f32[3,512,768]{2,1,0:T(8,128)}, bf16[8,2,256,256]{3,2,1,0:T(8,128)(2,1)}, f32[256,256]{1,0:T(8,128)}) custom-call(s32[3]{0:T(128)} %rows.1, s32[3]{0:T(128)} %cols.1, s32[3]{0:T(128)} %compare_convert_fusion.live, bf16[2,512,768]{2,1,0:T(8,128)(2,1)} %copy-done.4, bf16[8,2,256,256]{3,2,1,0:T(8,128)(2,1)} %bitcast.6, f32[3,256,256]{2,1,0:T(8,128)} %meas.1, ...), custom_call_target="tpu_custom_call" | custom-call | tf_op jit(solution)/shard_map/refine/pallas_call | solution.py:266
  64.4 0.8 constant_dynamic-slice_fusion
  65.2 0.0 copy-done.3
  65.2 0.0 copy-start.1
  65.2 1.6 %copy-done.1 = bf16[8,2,256,256]{3,2,1,0:T(8,128)(2,1)S(1)} copy-done((bf16[8,2,256,256]{3,2,1,0:T(8,128)(2,1)S(1)}, bf16[8,2,256,256]{3,2,1,0:T(8,128)(2,1)}, u32[]{:S(2)}) %copy-start.1) | copy-done | bytes 2097176
  66.8 0.0 copy-start.6
  66.8 0.9 copy-done.6
  67.7 61.4 %spread.1 = (f32[2,128,512]{2,1,0:T(8,128)S(1)}, f32[4,4,256]{2,1,0:T(4,128)S(1)}) custom-call(f32[3,512,768]{2,1,0:T(8,128)} %get-tuple-element.11.grad, bf16[4,4,256,256]{3,2,1,0:T(8,128)(2,1)S(1)} %bitcast.7, f32[256,256]{1,0:T(8,128)S(1)} %copy-done.6, f32[2,128,512]{2,1,0:T(8,128)S(1)} %copy-done.3, f32[4,4,256]{2,1,0:T(4,128)S(1)} %bitcast.8), custom_call_target="tpu_custom_call" | custom-call | tf_op jit(solution)/shard_map/spread/pallas_call | solution.py:390
  129.1 0.8 copy.13
  129.9 0.6 copy.14
Async XLA Ops:
  1.8 1.0 copy-start.2
  2.8 1.2 copy-start.5
  33.3 1.4 %copy-start = (bf16[4,4,256,256]{3,2,1,0:T(8,128)(2,1)}, bf16[4,4,256,256]{3,2,1,0:T(8,128)(2,1)S(1)}, u32[]{:S(2)}) copy-start(bf16[4,4,256,256]{3,2,1,0:T(8,128)(2,1)S(1)} %get-tuple-element.10) | copy-start | bytes 6291460
  34.7 1.2 copy-start.4
  35.9 29.3 %copy-start.3 = (f32[2,128,512]{2,1,0:T(8,128)S(1)}, f32[2,128,512]{2,1,0:T(8,128)}, u32[]{:S(2)}) copy-start(f32[2,128,512]{2,1,0:T(8,128)} %obj.3) | copy-start | bytes 1572868
  65.2 1.6 %copy-start.1 = (bf16[8,2,256,256]{3,2,1,0:T(8,128)(2,1)S(1)}, bf16[8,2,256,256]{3,2,1,0:T(8,128)(2,1)}, u32[]{:S(2)}) copy-start(bf16[8,2,256,256]{3,2,1,0:T(8,128)(2,1)} %get-tuple-element.12) | copy-start | bytes 6291460
  66.8 0.9 copy-start.6

commit v3 on v2

v3 whole, which is shorter than its diff:
```python
import functools

import jax
import jax.numpy as jnp
import ml_dtypes
import numpy as np
from jax import lax
from jax.experimental import pallas as pl
from jax.experimental.pallas import tpu as pltpu
from jax.sharding import PartitionSpec as P

object_reg = 0.5
probe_reg = 1.0
N = 256
X, Y, Z = 4, 4, 8
bf = jnp.bfloat16
f32 = jnp.float32
MESH = pl.DeviceIdType.MESH
XY = [(i, j) for i in range(X) for j in range(Y) if i or j]


def tables():
    pos = np.arange(N)
    ang = (pos[:, None] * pos[None, :] % N) * (2.0 * np.pi / N)
    sc = 1.0 / np.sqrt(float(N))
    re = (np.cos(ang) * sc).astype(ml_dtypes.bfloat16)
    im = (-np.sin(ang) * sc).astype(ml_dtypes.bfloat16)
    forward = np.block([[re, im], [-im, re]]).astype(ml_dtypes.bfloat16)
    inverse = np.block([[re, -im], [im, re]]).astype(ml_dtypes.bfloat16)
    return forward, inverse


def dot(a, b):
    return jnp.dot(a, b, preferred_element_type=f32)


def here():
    tile = lax.axis_index("tile")
    group = lax.axis_index("mode")
    x = (group // 2) * 2 + tile // (Y * Z)
    return tile, group, x, (tile // Z) % Y, tile % Z, group % 2


def device(x, y, z, core):
    return {"tile": (x % 2) * (Y * Z) + y * Z + z, "mode": (x // 2) * 2 + core}


def greet(partners):
    barrier = pltpu.get_barrier_semaphore()
    for partner in partners:
        pl.semaphore_signal(barrier, inc=1, device_id=partner, device_id_type=MESH)
    pl.semaphore_wait(barrier, len(partners))


def sender(send_sem, recv_sem):
    def make(index, src, dst, target):
        return pltpu.make_async_remote_copy(
            src_ref=src, dst_ref=dst, send_sem=send_sem.at[index], recv_sem=recv_sem.at[index],
            device_id=target, device_id_type=MESH,
        )
    return make


def gather_kernel(obj, probe, ext, modes, block, send_sem, recv_sem):
    tile, group, x, y, z, core = here()
    tiles = X * Y * Z // 2
    sibling = device(x, y, z, 1 - core)
    opposite = device((x + 2) % X, y, z, core)
    across = device(X - 1 - x, y, z, core)
    along_y = [device(x, (y + i) % Y, z, core) for i in (1, 3, 2)]
    before, after = (tile + tiles - 1) % tiles, (tile + 1) % tiles
    other = (group + 2) % 4
    halo_to = [
        {"tile": before, "mode": group}, {"tile": before, "mode": other},
        {"tile": after, "mode": group}, {"tile": after, "mode": other},
    ]
    block[...] = obj[...].astype(bf)
    for k in range(2):
        for c in range(2):
            modes[group, 2 * k + c] = probe[k, c].astype(bf)
    mine = pl.multiple_of(group * 128, 128)
    theirs = pl.multiple_of(other * 128, 128)
    ext[:, pl.ds(mine, 128), 128:640] = block[...]

    @pl.when(tile == 0)
    def _():
        ext[:, :, :128] = jnp.zeros((2, 512, 128), bf)

    @pl.when(tile == tiles - 1)
    def _():
        ext[:, :, 640:] = jnp.zeros((2, 512, 128), bf)

    greet([sibling, opposite, across] + along_y + halo_to)
    make = sender(send_sem, recv_sem)

    def rows(start, low, width):
        return ext.at[:, pl.ds(start, 128), pl.ds(low, width)]

    def plane(which, index):
        return modes.at[which, pl.ds(index, 1)]

    far = make(0, block, rows(mine, 128, 512), opposite)
    far.start()
    cut = make(1, plane(group, y), plane(group, y), across)
    cut.start()
    left, right = block.at[:, :, pl.ds(0, 128)], block.at[:, :, pl.ds(384, 128)]
    halo = [
        make(2, left, rows(mine, 640, 128), halo_to[0]),
        make(3, left, rows(mine, 640, 128), halo_to[1]),
        make(4, right, rows(mine, 0, 128), halo_to[2]),
        make(5, right, rows(mine, 0, 128), halo_to[3]),
    ]
    sends = (tile > 0, tile > 0, tile < tiles - 1, tile < tiles - 1)
    gets = (tile < tiles - 1, tile < tiles - 1, tile > 0, tile > 0)
    for flag, copy in zip(sends, halo):
        pl.when(flag)(copy.start)
    near = make(6, block, rows(mine, 128, 512), sibling)
    near.start()
    own = make(7, modes.at[group], modes.at[group], sibling)
    own.start()

    passed = []

    def pass_on(index, ref):
        copy = make(index, ref, ref, sibling)
        copy.start()
        passed.append(copy)

    cut.wait_recv()
    spread = []
    for i, target in enumerate(along_y):
        copy = make(8 + i, plane(other, y), plane(other, y), target)
        copy.start()
        spread.append(copy)
    pass_on(11, plane(other, y))
    halo_kept = []
    for i, (flag, start, low) in enumerate(
        zip(gets, (mine, theirs, mine, theirs), (640, 640, 0, 0))
    ):
        on = make(12 + i, rows(start, low, 128), rows(start, low, 128), sibling)
        halo_kept.append((flag, on))

        @pl.when(flag)
        def _():
            halo[i].wait_recv()
            on.start()
    far.wait_recv()
    pass_on(16, rows(theirs, 128, 512))
    for i, step in enumerate((1, 3, 2)):
        spread[i].wait_recv()
        pass_on(17 + i, plane(other, (y + Y - step) % Y))
    for copy in [near, own] + passed:
        copy.wait()
    for copy in [far, cut] + spread:
        copy.wait_send()
    for flag, copy in zip(sends, halo):
        pl.when(flag)(copy.wait_send)
    for flag, copy in halo_kept:
        pl.when(flag)(copy.wait)


def gather(obj, probe):
    whole = pl.BlockSpec(memory_space=pltpu.VMEM)
    return pl.pallas_call(
        gather_kernel,
        out_shape=(
            jax.ShapeDtypeStruct((2, 512, 768), bf), jax.ShapeDtypeStruct((4, 4, N, N), bf)
        ),
        in_specs=[whole, whole],
        out_specs=(whole, whole),
        scratch_shapes=[
            pltpu.VMEM((2, 128, 512), bf),
            pltpu.SemaphoreType.DMA((20,)), pltpu.SemaphoreType.DMA((20,)),
        ],
        compiler_params=pltpu.CompilerParams(
            collective_id=0, has_side_effects=True, vmem_limit_bytes=40 * 2**20
        ),
        name="gather",
    )(obj, probe)


def refine_kernel(rows, cols, ext, probe, meas, fwd, inv, obj, probe_rows, object_out, probe_out,
                  patch, factor, spec, light, terms, to_cols, total, grads, sums,
                  out_probe, got_probe, out_power, got_power, pieces, got_piece, bands, got_band,
                  out_light, got_light, far_light, far_got_light, halo_light, halo_got_light,
                  out_grad, got_grad, far_grad, far_got_grad, halo_grad, halo_got_grad,
                  send_sem, recv_sem):
    tile, group, x, y, z, core = here()
    tiles = X * Y * Z // 2
    x_hi = group // 2
    sibling = device(x, y, z, 1 - core)
    opposite = device((x + 2) % X, y, z, core)
    before, after = (tile + tiles - 1) % tiles, (tile + 1) % tiles
    other = (group + 2) % 4
    halo_to = [
        {"tile": before, "mode": group}, {"tile": before, "mode": other},
        {"tile": after, "mode": group}, {"tile": after, "mode": other},
    ]
    in_plane = [device((x + i) % X, (y + j) % Y, z, core) for i, j in XY]
    along_z = [device(x, y, (z + i) % Z, core) for i in range(1, Z)]
    make = sender(send_sem, recv_sem)
    slots = 3

    greet([sibling] + halo_to + in_plane + along_z)

    light[...] = jnp.zeros_like(light)
    factor[0] = jnp.zeros((N, N), f32)

    def picks(height, width, shift, down):
        high = lax.broadcasted_iota(jnp.int32, (height, width), 0)
        wide = lax.broadcasted_iota(jnp.int32, (height, width), 1)
        hit = high == wide + shift if down else wide == high + shift
        return jnp.where(hit, 1.0, 0.0).astype(bf)

    def mode_light(g, _):
        for k in range(2):
            re = probe[g, 2 * k].astype(f32)
            im = probe[g, 2 * k + 1].astype(f32)
            light[...] += re * re + im * im
        return 0
    lax.fori_loop(0, 4, mode_light, 0)

    def scatter(c):
        spread_rows = [
            dot(picks(512, N, rows[s], True), terms[s]).astype(bf) for s in range(slots)
        ]
        for s in range(slots):
            to_cols[s * N:(s + 1) * N, :] = picks(N, 768, cols[s], False)
        total[c] = dot(jnp.concatenate(spread_rows, 1), to_cols[...])

    for s in range(slots):
        from_cols = picks(768, N, cols[s], True)
        from_rows = picks(N, 512, rows[s], False)
        for c in range(2):
            strip = dot(ext[c], from_cols).astype(bf)
            patch[s, c] = dot(from_rows, strip)
        factor[0] += patch[s, 0] * patch[s, 0] + patch[s, 1] * patch[s, 1]
        terms[s] = light[...].astype(bf)
    scatter(0)
    out_power[...] = factor[0].astype(bf)
    power_copy = make(0, out_power, got_power, sibling)
    power_copy.start()

    def sibling_rows(c, out, k):
        for h in range(2):
            start = pl.multiple_of((2 * h + 1 - core) * 128, 128)
            out[h, k] = total[c, pl.ds(start, 128), :].astype(bf)

    def own_rows(c, h, got, k):
        start = pl.multiple_of((2 * h + core) * 128, 128)
        return total[c, pl.ds(start, 128), :] + got[h, k].astype(f32)

    def fan_out(first, far, far_got, halo, halo_got):
        copies = [
            make(first, far.at[:, :, pl.ds(128, 512)], far_got, opposite),
            make(first + 1, halo.at[0], halo_got.at[0], halo_to[0]),
            make(first + 2, far.at[:, :, pl.ds(0, 128)], halo_got.at[1], halo_to[1]),
            make(first + 3, halo.at[1], halo_got.at[2], halo_to[2]),
            make(first + 4, far.at[:, :, pl.ds(640, 128)], halo_got.at[3], halo_to[3]),
        ]
        for copy in copies:
            copy.start()
        return copies

    keep_left = jnp.where(tile > 0, 1.0, 0.0)
    keep_right = jnp.where(tile < tiles - 1, 1.0, 0.0)

    def merged(kept, far_got, halo_got, k):
        center = kept[:, 128:640] + far_got[k].astype(f32)
        from_right = (halo_got[0, k].astype(f32) + halo_got[1, k].astype(f32)) * keep_right
        from_left = (halo_got[2, k].astype(f32) + halo_got[3, k].astype(f32)) * keep_left
        return jnp.concatenate(
            [center[:, :128] + from_left, center[:, 128:384], center[:, 384:] + from_right], 1
        )

    sibling_rows(0, out_light, 0)
    light_copy = make(1, out_light, got_light, sibling)
    light_copy.start()

    def spectra(s, _):
        power = jnp.zeros((N, N), f32)
        ar = patch[s, 0]
        ai = patch[s, 1]
        for m in range(8):
            pr = probe[m // 2, 2 * (m % 2)].astype(f32)
            pi = probe[m // 2, 2 * (m % 2) + 1].astype(f32)
            wave = jnp.concatenate([pr * ar - pi * ai, pr * ai + pi * ar], 1).astype(bf)
            half = dot(wave, fwd[...]).astype(bf)
            spectrum = dot(inv[...], jnp.concatenate([half[:, :N], half[:, N:]], 0))
            spec[s, m] = spectrum
            power = power + spectrum[:N] * spectrum[:N] + spectrum[N:] * spectrum[N:]
        factor[s] = meas[s] * lax.rsqrt(jnp.maximum(power, 0.25)) - 1.0
        return 0
    lax.fori_loop(0, slots, spectra, 0)

    light_copy.wait_recv()
    kept_light = own_rows(0, x_hi, got_light, 0)
    far_light[0] = own_rows(0, 1 - x_hi, got_light, 0).astype(bf)
    halo_light[0, 0] = kept_light[:, :128].astype(bf)
    halo_light[1, 0] = kept_light[:, 640:].astype(bf)
    light_copies = fan_out(2, far_light, far_got_light, halo_light, halo_got_light)
    power_copy.wait_recv()
    total_power = (out_power[...].astype(f32) + got_power[...].astype(f32)).astype(bf)
    pieces[0, 4] = total_power
    pieces[1, 4] = total_power

    grads[...] = jnp.zeros_like(grads)

    def passed(q):
        return make(7 + q, out_probe.at[q], got_probe.at[q], sibling)

    def piece(h, xl, j):
        i = (2 * h + xl - x + X) % X
        k = i * Y + j
        start = pl.multiple_of(xl * 128 + ((y + j) % Y) * 32, 32)
        copy = make(
            9 + k, pieces.at[h, :, pl.ds(start, 32), :], got_piece.at[k],
            device(2 * h + xl, (y + j) % Y, z, core),
        )
        return copy, k

    def back_step(q, _):
        h = q % 2
        side = jnp.where(q < 2, 1 - core, core)
        g = 2 * h + side
        sums[...] = jnp.zeros_like(sums)
        for s in range(slots):
            fac = factor[s]
            ar = patch[s, 0]
            ai = patch[s, 1]
            for k in range(2):
                spectrum = spec[s, 2 * g + k]
                diff = jnp.concatenate([spectrum[:N] * fac, spectrum[N:] * fac], 0).astype(bf)
                half = dot(fwd[...], diff).astype(bf)
                back = dot(jnp.concatenate([half[:N], half[N:]], 1), inv[...])
                br = back[:, :N]
                bi = back[:, N:]
                pr = probe[g, 2 * k].astype(f32)
                pi = probe[g, 2 * k + 1].astype(f32)
                sums[2 * k] += ar * br + ai * bi
                sums[2 * k + 1] += ar * bi - ai * br
                grads[s, 0] += pr * br + pi * bi
                grads[s, 1] += pr * bi - pi * br

        @pl.when(q < 2)
        def _():
            out_probe[h] = sums[...].astype(bf)
            passed(h).start()

        @pl.when(q >= 2)
        def _():
            passed(h).wait_recv()
            for k in range(4):
                pieces[h, k] = (sums[k] + got_probe[h, k].astype(f32)).astype(bf)
            for xl in range(2):
                for j in range(Y):
                    copy, k = piece(h, xl, j)
                    if j:
                        copy.start()
                    else:
                        pl.when(k > 0)(copy.start)
        return 0
    lax.fori_loop(0, 4, back_step, 0)

    for copy in light_copies:
        copy.wait_recv()
    weight = merged(kept_light, far_got_light, halo_got_light, 0) + object_reg

    for c in range(2):
        for s in range(slots):
            terms[s] = grads[s, c].astype(bf)
        scatter(c)
    for c in range(2):
        sibling_rows(c, out_grad, c)
    grad_copy = make(32, out_grad, got_grad, sibling)
    grad_copy.start()

    band_start = pl.multiple_of((x % 2) * 128 + y * 32, 32)
    band = pieces[x_hi, :, pl.ds(band_start, 32), :].astype(f32)
    grad_copy.wait_recv()
    for c in range(2):
        far_grad[c] = own_rows(c, 1 - x_hi, got_grad, c).astype(bf)
        halo_grad[0, c] = own_rows(c, x_hi, got_grad, c)[:, :128].astype(bf)
        halo_grad[1, c] = own_rows(c, x_hi, got_grad, c)[:, 640:].astype(bf)
    grad_copies = fan_out(33, far_grad, far_got_grad, halo_grad, halo_got_grad)

    def arrived(k):
        return make(9 + k, pieces.at[0, :, pl.ds(0, 32), :], got_piece.at[k], sibling)
    for k in range(1, X * Y):
        arrived(k).wait_recv()
        band = band + got_piece[k].astype(f32)
    for part in range(Z):
        for k in range(5):
            bands[part, 4 * k:4 * k + 4] = band[k, 4 * part:4 * part + 4]
    band_copies = []
    for i in range(1, Z):
        copy = make(24 + i, bands.at[(z + i) % Z], got_band.at[i - 1], along_z[i - 1])
        copy.start()
        band_copies.append(copy)

    for copy in grad_copies:
        copy.wait_recv()
    for c in range(2):
        kept = own_rows(c, x_hi, got_grad, c)
        object_out[c] = obj[c] + merged(kept, far_got_grad, halo_got_grad, c) / weight

    final = bands[z]
    for i in range(Z - 1):
        band_copies[i].wait_recv()
        final = final + got_band[i]
    weight = final[16:20] + probe_reg
    for k in range(4):
        probe_out[k] = probe_rows[k] + final[4 * k:4 * k + 4] / weight
    for copy in [power_copy, light_copy, grad_copy, passed(0), passed(1)] + light_copies + grad_copies + band_copies:
        copy.wait_send()
    for k in range(1, X * Y):
        arrived(k).wait_send()


def refine(rows, cols, ext, probe, meas, obj, probe_rows):
    forward, inverse = tables()
    whole = pl.BlockSpec(memory_space=pltpu.VMEM)
    scalars = pl.BlockSpec(memory_space=pltpu.SMEM)
    return pl.pallas_call(
        refine_kernel,
        out_shape=(
            jax.ShapeDtypeStruct((2, 128, 512), f32), jax.ShapeDtypeStruct((4, 4, N), f32)
        ),
        in_specs=[scalars] * 2 + [whole] * 7,
        out_specs=(whole, whole),
        scratch_shapes=[
            pltpu.VMEM((3, 2, N, N), f32),
            pltpu.VMEM((3, N, N), f32),
            pltpu.VMEM((3, 8, 2 * N, N), f32),
            pltpu.VMEM((N, N), f32),
            pltpu.VMEM((3, N, N), bf),
            pltpu.VMEM((3 * N, 768), bf),
            pltpu.VMEM((2, 512, 768), f32),
            pltpu.VMEM((3, 2, N, N), f32),
            pltpu.VMEM((4, N, N), f32),
            pltpu.VMEM((2, 4, N, N), bf),
            pltpu.VMEM((2, 4, N, N), bf),
            pltpu.VMEM((N, N), bf),
            pltpu.VMEM((N, N), bf),
            pltpu.VMEM((2, 5, N, N), bf),
            pltpu.VMEM((X * Y, 5, 32, N), bf),
            pltpu.VMEM((Z, 24, N), f32),
            pltpu.VMEM((Z - 1, 24, N), f32),
            pltpu.VMEM((2, 1, 128, 768), bf),
            pltpu.VMEM((2, 1, 128, 768), bf),
            pltpu.VMEM((1, 128, 768), bf),
            pltpu.VMEM((1, 128, 512), bf),
            pltpu.VMEM((2, 1, 128, 128), bf),
            pltpu.VMEM((4, 1, 128, 128), bf),
            pltpu.VMEM((2, 2, 128, 768), bf),
            pltpu.VMEM((2, 2, 128, 768), bf),
            pltpu.VMEM((2, 128, 768), bf),
            pltpu.VMEM((2, 128, 512), bf),
            pltpu.VMEM((2, 2, 128, 128), bf),
            pltpu.VMEM((4, 2, 128, 128), bf),
            pltpu.SemaphoreType.DMA((40,)), pltpu.SemaphoreType.DMA((40,)),
        ],
        compiler_params=pltpu.CompilerParams(
            collective_id=1, has_side_effects=True, vmem_limit_bytes=60 * 2**20
        ),
        name="refine",
    )(rows, cols, ext, probe, meas, jnp.asarray(forward), jnp.asarray(inverse), obj, probe_rows)


def local(object_field, probe, measured, scan_rows, scan_cols, counts):
    slots = scan_rows.shape[0]
    first_slot = lax.axis_index("mode") * slots
    live = first_slot + jnp.arange(slots, dtype=jnp.int32) < counts[0]
    live_rows = jnp.where(live, scan_rows, 4096)
    extended, probe_all = gather(object_field, probe)
    probe_rows = lax.dynamic_slice_in_dim(probe, lax.axis_index("tile") * 4, 4, 2)
    object_out, probe_out = refine(
        live_rows, scan_cols, extended, probe_all, measured, object_field,
        probe_rows.reshape(4, 4, N),
    )
    return object_out, probe_out.reshape(2, 2, 4, N)


def solution(mesh):
    return jax.shard_map(
        local,
        mesh=mesh,
        in_specs=(
            P(None, "mode", "tile"),
            P("mode", None, None, None),
            P(("tile", "mode"), None, None),
            P(("tile", "mode")),
            P(("tile", "mode")),
            P("tile"),
        ),
        out_specs=(P(None, "mode", "tile"), P("mode", None, "tile", None)),
        check_vma=False,
    )
```

time: 131 us -> 108 us (0.82)
  the two profiles are of different devices: /device:TPU:16 before, /device:TPU:6 now
where the time goes in v3:
time: 108 us
  Pallas kernels  96 us (89%)
  local copies, waits for them, and re-layouts  9.31 us (9%)
  between operations  1.31 us (1%)
  other arithmetic  1.17 us (1%)
    pallas_call x1, Pallas kernels, refine(): pl.pallas_call(refine_kernel, out_shape=(jax.ShapeDtypeStruct((2, 128, 51...  65.4 us
    pallas_call x1, Pallas kernels, gather(): pl.pallas_call(gather_kernel, out_shape=(jax.ShapeDtypeStruct((2, 512, 76...  30.5 us
    unnamed x10, local copies, waits for them, and re-layouts  7.95 us

profile of v3, /device:TPU:6, one launch (start us, length us, event | category | flops | bytes accessed | tf_op | source)
XLA Modules:
  0.0 107.8 jit_solution(10074565294279659156)
XLA Ops:
  1.3 1.2 %compare_select_fusion.rows = s32[3]{0:T(128)} fusion(s32[3]{0:T(128)} %param.11, s32[]{:T(128)} %bitcast.3, s32[]{:T(128)S(6)} %mul.6), kind=kLoop, calls=%fused_computation | loop fusion | flops 9 | bytes 32 | tf_op jit(solution)/shard_map/jit(_where)/select_n | solution.py:474
  2.5 1.4 %constant_dynamic-slice_fusion = f32[2,2,4,256]{3,2,1,0:T(4,128)} fusion(f32[2,2,256,256]{3,2,1,0:T(8,128)} %probe.1, s32[]{:T(128)S(6)} %select_n.8), kind=kLoop, calls=%fused_computation.1 | loop fusion | bytes 32772 | tf_op jit(solution)/shard_map/dynamic_slice | solution.py:476
  3.8 0.0 copy-start.1
  3.8 1.0 copy-done.1
  4.9 0.0 copy-start.3
  4.9 1.2 %copy-done.3 = f32[2,2,256,256]{3,2,1,0:T(8,128)S(1)} copy-done((f32[2,2,256,256]{3,2,1,0:T(8,128)S(1)}, f32[2,2,256,256]{3,2,1,0:T(8,128)}, u32[]{:S(2)}) %copy-start.3) | copy-done | bytes 1048600
  6.1 30.5 %gather.1 = (bf16[2,512,768]{2,1,0:T(8,128)(2,1)S(1)}, bf16[4,4,256,256]{3,2,1,0:T(8,128)(2,1)S(1)}) custom-call(f32[2,128,512]{2,1,0:T(8,128)S(1)} %copy-done.1, f32[2,2,256,256]{3,2,1,0:T(8,128)S(1)} %copy-done.3), custom_call_target="tpu_custom_call" | custom-call | tf_op jit(solution)/shard_map/gather/pallas_call | solution.py:164
  36.6 0.0 copy-start
  36.6 1.3 %copy-done = bf16[4,4,256,256]{3,2,1,0:T(8,128)(2,1)} copy-done((bf16[4,4,256,256]{3,2,1,0:T(8,128)(2,1)}, bf16[4,4,256,256]{3,2,1,0:T(8,128)(2,1)S(1)}, u32[]{:S(2)}) %copy-start) | copy-done | bytes 2097176
  38.0 0.0 copy-start.2
  38.0 1.2 %copy-done.2 = bf16[2,512,768]{2,1,0:T(8,128)(2,1)} copy-done((bf16[2,512,768]{2,1,0:T(8,128)(2,1)}, bf16[2,512,768]{2,1,0:T(8,128)(2,1)S(1)}, u32[]{:S(2)}) %copy-start.2) | copy-done | bytes 1572888
  39.1 65.4 %refine.1 = (f32[2,128,512]{2,1,0:T(8,128)}, f32[4,4,256]{2,1,0:T(4,128)}) custom-call(s32[3]{0:T(128)} %compare_select_fusion.rows, s32[3]{0:T(128)} %cols.1, bf16[2,512,768]{2,1,0:T(8,128)(2,1)} %copy-done.2, bf16[4,4,256,256]{3,2,1,0:T(8,128)(2,1)} %copy-done, f32[3,256,256]{2,1,0:T(8,128)} %meas.1, bf16[512,512]{1,0:T(8,128)(2,1)} %constant.23.clone.fwd, ...), custom_call_target="tpu_custom_call" | custom-call | tf_op jit(solution)/shard_map/refine/pallas_call | solution.py:424
  104.6 1.9 %copy.13 = f32[2,128,512]{2,1,0:T(8,128)} copy(f32[2,128,512]{2,1,0:T(8,128)} %get-tuple-element.12) | data formatting | bytes 1048576
  106.5 1.3 %copy.14 = f32[2,2,4,256]{3,2,1,0:T(4,128)} copy(f32[2,2,4,256]{3,2,1,0:T(4,128)} %bitcast.5) | data formatting | bytes 32768
Async XLA Ops:
  3.8 1.0 copy-start.1
  4.9 1.2 %copy-start.3 = (f32[2,2,256,256]{3,2,1,0:T(8,128)S(1)}, f32[2,2,256,256]{3,2,1,0:T(8,128)}, u32[]{:S(2)}) copy-start(f32[2,2,256,256]{3,2,1,0:T(8,128)} %probe.1) | copy-start | bytes 3145732
  36.6 1.3 %copy-start = (bf16[4,4,256,256]{3,2,1,0:T(8,128)(2,1)}, bf16[4,4,256,256]{3,2,1,0:T(8,128)(2,1)S(1)}, u32[]{:S(2)}) copy-start(bf16[4,4,256,256]{3,2,1,0:T(8,128)(2,1)S(1)} %get-tuple-element.7.probe) | copy-start | bytes 6291460
  38.0 1.2 %copy-start.2 = (bf16[2,512,768]{2,1,0:T(8,128)(2,1)}, bf16[2,512,768]{2,1,0:T(8,128)(2,1)S(1)}, u32[]{:S(2)}) copy-start(bf16[2,512,768]{2,1,0:T(8,128)(2,1)S(1)} %get-tuple-element.6.ext) | copy-start | bytes 4718596

commit v4 on v3

--- a/solution.py
+++ b/solution.py
@@ -61,130 +61,22 @@
     return make
 
 
-def gather_kernel(obj, probe, ext, modes, block, send_sem, recv_sem):
-    tile, group, x, y, z, core = here()
-    tiles = X * Y * Z // 2
-    sibling = device(x, y, z, 1 - core)
-    opposite = device((x + 2) % X, y, z, core)
-    across = device(X - 1 - x, y, z, core)
-    along_y = [device(x, (y + i) % Y, z, core) for i in (1, 3, 2)]
-    before, after = (tile + tiles - 1) % tiles, (tile + 1) % tiles
-    other = (group + 2) % 4
-    halo_to = [
-        {"tile": before, "mode": group}, {"tile": before, "mode": other},
-        {"tile": after, "mode": group}, {"tile": after, "mode": other},
-    ]
-    block[...] = obj[...].astype(bf)
-    for k in range(2):
-        for c in range(2):
-            modes[group, 2 * k + c] = probe[k, c].astype(bf)
-    mine = pl.multiple_of(group * 128, 128)
-    theirs = pl.multiple_of(other * 128, 128)
-    ext[:, pl.ds(mine, 128), 128:640] = block[...]
-
-    @pl.when(tile == 0)
-    def _():
-        ext[:, :, :128] = jnp.zeros((2, 512, 128), bf)
-
-    @pl.when(tile == tiles - 1)
-    def _():
-        ext[:, :, 640:] = jnp.zeros((2, 512, 128), bf)
-
-    greet([sibling, opposite, across] + along_y + halo_to)
-    make = sender(send_sem, recv_sem)
-
-    def rows(start, low, width):
-        return ext.at[:, pl.ds(start, 128), pl.ds(low, width)]
-
-    def plane(which, index):
-        return modes.at[which, pl.ds(index, 1)]
-
-    far = make(0, block, rows(mine, 128, 512), opposite)
-    far.start()
-    cut = make(1, plane(group, y), plane(group, y), across)
-    cut.start()
-    left, right = block.at[:, :, pl.ds(0, 128)], block.at[:, :, pl.ds(384, 128)]
-    halo = [
-        make(2, left, rows(mine, 640, 128), halo_to[0]),
-        make(3, left, rows(mine, 640, 128), halo_to[1]),
-        make(4, right, rows(mine, 0, 128), halo_to[2]),
-        make(5, right, rows(mine, 0, 128), halo_to[3]),
-    ]
-    sends = (tile > 0, tile > 0, tile < tiles - 1, tile < tiles - 1)
-    gets = (tile < tiles - 1, tile < tiles - 1, tile > 0, tile > 0)
-    for flag, copy in zip(sends, halo):
-        pl.when(flag)(copy.start)
-    near = make(6, block, rows(mine, 128, 512), sibling)
-    near.start()
-    own = make(7, modes.at[group], modes.at[group], sibling)
-    own.start()
-
-    passed = []
-
-    def pass_on(index, ref):
-        copy = make(index, ref, ref, sibling)
-        copy.start()
-        passed.append(copy)
-
-    cut.wait_recv()
-    spread = []
-    for i, target in enumerate(along_y):
-        copy = make(8 + i, plane(other, y), plane(other, y), target)
-        copy.start()
-        spread.append(copy)
-    pass_on(11, plane(other, y))
-    halo_kept = []
-    for i, (flag, start, low) in enumerate(
-        zip(gets, (mine, theirs, mine, theirs), (640, 640, 0, 0))
-    ):
-        on = make(12 + i, rows(start, low, 128), rows(start, low, 128), sibling)
-        halo_kept.append((flag, on))
-
-        @pl.when(flag)
-        def _():
-            halo[i].wait_recv()
-            on.start()
-    far.wait_recv()
-    pass_on(16, rows(theirs, 128, 512))
-    for i, step in enumerate((1, 3, 2)):
-        spread[i].wait_recv()
-        pass_on(17 + i, plane(other, (y + Y - step) % Y))
-    for copy in [near, own] + passed:
-        copy.wait()
-    for copy in [far, cut] + spread:
-        copy.wait_send()
-    for flag, copy in zip(sends, halo):
-        pl.when(flag)(copy.wait_send)
-    for flag, copy in halo_kept:
-        pl.when(flag)(copy.wait)
-
-
-def gather(obj, probe):
-    whole = pl.BlockSpec(memory_space=pltpu.VMEM)
-    return pl.pallas_call(
-        gather_kernel,
-        out_shape=(
-            jax.ShapeDtypeStruct((2, 512, 768), bf), jax.ShapeDtypeStruct((4, 4, N, N), bf)
-        ),
-        in_specs=[whole, whole],
-        out_specs=(whole, whole),
-        scratch_shapes=[
-            pltpu.VMEM((2, 128, 512), bf),
-            pltpu.SemaphoreType.DMA((20,)), pltpu.SemaphoreType.DMA((20,)),
-        ],
-        compiler_params=pltpu.CompilerParams(
-            collective_id=0, has_side_effects=True, vmem_limit_bytes=40 * 2**20
-        ),
-        name="gather",
-    )(obj, probe)
-
-
-def refine_kernel(rows, cols, ext, probe, meas, fwd, inv, obj, probe_rows, object_out, probe_out,
+def refine_kernel(counts, rows_in, cols, obj_in, probe_in, meas_in, fwd_in, inv_in, object_out, probe_out,
+                  obj, probe, meas, fwd, inv, block, ext, modes, powers,
                   patch, factor, spec, light, terms, to_cols, total, grads, sums,
                   out_probe, got_probe, out_power, got_power, pieces, got_piece, bands, got_band,
                   out_light, got_light, far_light, far_got_light, halo_light, halo_got_light,
                   out_grad, got_grad, far_grad, far_got_grad, halo_grad, halo_got_grad,
-                  send_sem, recv_sem):
+                  send_sem, recv_sem, load_sem):
+    loads = [
+        pltpu.make_async_copy(src, dst, load_sem.at[i])
+        for i, (src, dst) in enumerate(
+            ((obj_in, obj), (probe_in, probe), (fwd_in, fwd), (inv_in, inv), (meas_in, meas))
+        )
+    ]
+    for load in loads:
+        load.start()
+    slots = 3
     tile, group, x, y, z, core = here()
     tiles = X * Y * Z // 2
     x_hi = group // 2
@@ -199,9 +91,90 @@
     in_plane = [device((x + i) % X, (y + j) % Y, z, core) for i, j in XY]
     along_z = [device(x, y, (z + i) % Z, core) for i in range(1, Z)]
     make = sender(send_sem, recv_sem)
-    slots = 3
-
-    greet([sibling] + halo_to + in_plane + along_z)
+
+    across = device(X - 1 - x, y, z, core)
+    along_y = [device(x, (y + i) % Y, z, core) for i in (1, 3, 2)]
+    partners = [sibling] + halo_to + in_plane + along_z
+    barrier = pltpu.get_barrier_semaphore()
+    for partner in partners:
+        pl.semaphore_signal(barrier, inc=1, device_id=partner, device_id_type=MESH)
+    rows = [jnp.where(group * slots + s < counts[0], rows_in[s], 4096) for s in range(slots)]
+
+    mine = pl.multiple_of(group * 128, 128)
+    theirs = pl.multiple_of(other * 128, 128)
+    loads[0].wait()
+    block[...] = obj[...].astype(bf)
+    ext[:, pl.ds(mine, 128), 128:640] = block[...]
+
+    @pl.when(tile == 0)
+    def _():
+        ext[:, :, :128] = jnp.zeros((2, 512, 128), bf)
+
+    @pl.when(tile == tiles - 1)
+    def _():
+        ext[:, :, 640:] = jnp.zeros((2, 512, 128), bf)
+
+    loads[1].wait()
+    for k in range(2):
+        for c in range(2):
+            modes[group, 2 * k + c] = probe[k, c].astype(bf)
+    pl.semaphore_wait(barrier, len(partners))
+
+    def strip(start, low, width):
+        return ext.at[:, pl.ds(start, 128), pl.ds(low, width)]
+
+    def plane(which, index):
+        return modes.at[which, pl.ds(index, 1)]
+
+    far = make(40, block, strip(mine, 128, 512), opposite)
+    far.start()
+    left, right = block.at[:, :, pl.ds(0, 128)], block.at[:, :, pl.ds(384, 128)]
+    halo = [
+        make(42, left, strip(mine, 640, 128), halo_to[0]),
+        make(43, left, strip(mine, 640, 128), halo_to[1]),
+        make(44, right, strip(mine, 0, 128), halo_to[2]),
+        make(45, right, strip(mine, 0, 128), halo_to[3]),
+    ]
+    sends = (tile > 0, tile > 0, tile < tiles - 1, tile < tiles - 1)
+    gets = (tile < tiles - 1, tile < tiles - 1, tile > 0, tile > 0)
+    for flag, copy in zip(sends, halo):
+        pl.when(flag)(copy.start)
+    cut = make(41, plane(group, y), plane(group, y), across)
+    cut.start()
+    near = make(46, block, strip(mine, 128, 512), sibling)
+    near.start()
+    own = make(47, modes.at[group], modes.at[group], sibling)
+    own.start()
+
+    def pass_on(index, ref):
+        copy = make(index, ref, ref, sibling)
+        copy.start()
+        return copy
+
+    halo_kept = []
+    for i, (flag, start, low) in enumerate(
+        zip(gets, (mine, theirs, mine, theirs), (640, 640, 0, 0))
+    ):
+        on = make(52 + i, strip(start, low, 128), strip(start, low, 128), sibling)
+        halo_kept.append((flag, on))
+
+        @pl.when(flag)
+        def _():
+            halo[i].wait_recv()
+            on.start()
+    far.wait_recv()
+    far_on = pass_on(56, strip(theirs, 128, 512))
+    cut.wait_recv()
+    around = []
+    for i, target in enumerate(along_y):
+        copy = make(48 + i, plane(other, y), plane(other, y), target)
+        copy.start()
+        around.append(copy)
+    planes_on = [pass_on(51, plane(other, y))]
+    near.wait_recv()
+    far_on.wait_recv()
+    for flag, on in halo_kept:
+        pl.when(flag)(on.wait_recv)
 
     light[...] = jnp.zeros_like(light)
     factor[0] = jnp.zeros((N, N), f32)
@@ -211,14 +184,6 @@
         wide = lax.broadcasted_iota(jnp.int32, (height, width), 1)
         hit = high == wide + shift if down else wide == high + shift
         return jnp.where(hit, 1.0, 0.0).astype(bf)
-
-    def mode_light(g, _):
-        for k in range(2):
-            re = probe[g, 2 * k].astype(f32)
-            im = probe[g, 2 * k + 1].astype(f32)
-            light[...] += re * re + im * im
-        return 0
-    lax.fori_loop(0, 4, mode_light, 0)
 
     def scatter(c):
         spread_rows = [
@@ -232,11 +197,9 @@
         from_cols = picks(768, N, cols[s], True)
         from_rows = picks(N, 512, rows[s], False)
         for c in range(2):
-            strip = dot(ext[c], from_cols).astype(bf)
-            patch[s, c] = dot(from_rows, strip)
+            narrow = dot(ext[c], from_cols).astype(bf)
+            patch[s, c] = dot(from_rows, narrow)
         factor[0] += patch[s, 0] * patch[s, 0] + patch[s, 1] * patch[s, 1]
-        terms[s] = light[...].astype(bf)
-    scatter(0)
     out_power[...] = factor[0].astype(bf)
     power_copy = make(0, out_power, got_power, sibling)
     power_copy.start()
@@ -273,37 +236,57 @@
             [center[:, :128] + from_left, center[:, 128:384], center[:, 384:] + from_right], 1
         )
 
+    for i, step in enumerate((1, 3, 2)):
+        around[i].wait_recv()
+        planes_on.append(pass_on(57 + i, plane(other, (y + Y - step) % Y)))
+    loads[2].wait()
+    loads[3].wait()
+    powers[...] = jnp.zeros_like(powers)
+
+    def spectra(q, _):
+        g = jnp.where(q % 2 == 0, group, group + 1 - 2 * core)
+        g = jnp.where(q < 2, g, (g + 2) % 4)
+
+        @pl.when(q == 1)
+        def _():
+            own.wait_recv()
+
+        @pl.when(q == 3)
+        def _():
+            for copy in planes_on:
+                copy.wait_recv()
+
+        for s in range(slots):
+            ar = patch[s, 0]
+            ai = patch[s, 1]
+            for k in range(2):
+                pr = modes[g, 2 * k].astype(f32)
+                pi = modes[g, 2 * k + 1].astype(f32)
+                wave = jnp.concatenate([pr * ar - pi * ai, pr * ai + pi * ar], 1).astype(bf)
+                half = dot(wave, fwd[...]).astype(bf)
+                spectrum = dot(inv[...], jnp.concatenate([half[:, :N], half[:, N:]], 0))
+                spec[s, 2 * g + k] = spectrum
+                powers[s] += spectrum[:N] * spectrum[:N] + spectrum[N:] * spectrum[N:]
+        return 0
+    lax.fori_loop(0, 4, spectra, 0)
+    loads[4].wait()
+    for s in range(slots):
+        factor[s] = meas[s] * lax.rsqrt(jnp.maximum(powers[s], 0.25)) - 1.0
+
+    def mode_light(g, _):
+        for k in range(2):
+            re = modes[g, 2 * k].astype(f32)
+            im = modes[g, 2 * k + 1].astype(f32)
+            light[...] += re * re + im * im
+        return 0
+    lax.fori_loop(0, 4, mode_light, 0)
+
+    for s in range(slots):
+        terms[s] = light[...].astype(bf)
+    scatter(0)
     sibling_rows(0, out_light, 0)
     light_copy = make(1, out_light, got_light, sibling)
     light_copy.start()
-
-    def spectra(s, _):
-        power = jnp.zeros((N, N), f32)
-        ar = patch[s, 0]
-        ai = patch[s, 1]
-        for m in range(8):
-            pr = probe[m // 2, 2 * (m % 2)].astype(f32)
-            pi = probe[m // 2, 2 * (m % 2) + 1].astype(f32)
-            wave = jnp.concatenate([pr * ar - pi * ai, pr * ai + pi * ar], 1).astype(bf)
-            half = dot(wave, fwd[...]).astype(bf)
-            spectrum = dot(inv[...], jnp.concatenate([half[:, :N], half[:, N:]], 0))
-            spec[s, m] = spectrum
-            power = power + spectrum[:N] * spectrum[:N] + spectrum[N:] * spectrum[N:]
-        factor[s] = meas[s] * lax.rsqrt(jnp.maximum(power, 0.25)) - 1.0
-        return 0
-    lax.fori_loop(0, slots, spectra, 0)
-
-    light_copy.wait_recv()
-    kept_light = own_rows(0, x_hi, got_light, 0)
-    far_light[0] = own_rows(0, 1 - x_hi, got_light, 0).astype(bf)
-    halo_light[0, 0] = kept_light[:, :128].astype(bf)
-    halo_light[1, 0] = kept_light[:, 640:].astype(bf)
-    light_copies = fan_out(2, far_light, far_got_light, halo_light, halo_got_light)
-    power_copy.wait_recv()
-    total_power = (out_power[...].astype(f32) + got_power[...].astype(f32)).astype(bf)
-    pieces[0, 4] = total_power
-    pieces[1, 4] = total_power
-
     grads[...] = jnp.zeros_like(grads)
 
     def passed(q):
@@ -335,8 +318,8 @@
                 back = dot(jnp.concatenate([half[:N], half[N:]], 1), inv[...])
                 br = back[:, :N]
                 bi = back[:, N:]
-                pr = probe[g, 2 * k].astype(f32)
-                pi = probe[g, 2 * k + 1].astype(f32)
+                pr = modes[g, 2 * k].astype(f32)
+                pi = modes[g, 2 * k + 1].astype(f32)
                 sums[2 * k] += ar * br + ai * bi
                 sums[2 * k + 1] += ar * bi - ai * br
                 grads[s, 0] += pr * br + pi * bi
@@ -360,7 +343,19 @@
                     else:
                         pl.when(k > 0)(copy.start)
         return 0
-    lax.fori_loop(0, 4, back_step, 0)
+    lax.fori_loop(0, 1, back_step, 0)
+    light_copy.wait_recv()
+    kept_light = own_rows(0, x_hi, got_light, 0)
+    far_light[0] = own_rows(0, 1 - x_hi, got_light, 0).astype(bf)
+    halo_light[0, 0] = kept_light[:, :128].astype(bf)
+    halo_light[1, 0] = kept_light[:, 640:].astype(bf)
+    light_copies = fan_out(2, far_light, far_got_light, halo_light, halo_got_light)
+    power_copy.wait_recv()
+    total_power = (out_power[...].astype(f32) + got_power[...].astype(f32)).astype(bf)
+    pieces[0, 4] = total_power
+    pieces[1, 4] = total_power
+
+    lax.fori_loop(1, 4, back_step, 0)
 
     for copy in light_copies:
         copy.wait_recv()
@@ -409,26 +404,45 @@
         band_copies[i].wait_recv()
         final = final + got_band[i]
     weight = final[16:20] + probe_reg
+    at = pl.multiple_of((tile // 2) * 8, 8)
     for k in range(4):
-        probe_out[k] = probe_rows[k] + final[4 * k:4 * k + 4] / weight
+        rows8 = probe[k // 2, k % 2, pl.ds(at, 8), :]
+        probe_row = jnp.where(tile % 2 == 0, rows8[:4], rows8[4:])
+        probe_out[k] = probe_row + final[4 * k:4 * k + 4] / weight
+    for copy in [far, cut, near, own, far_on] + around + planes_on:
+        copy.wait_send()
+    for flag, copy in zip(sends, halo):
+        pl.when(flag)(copy.wait_send)
+    for flag, copy in halo_kept:
+        pl.when(flag)(copy.wait_send)
     for copy in [power_copy, light_copy, grad_copy, passed(0), passed(1)] + light_copies + grad_copies + band_copies:
         copy.wait_send()
     for k in range(1, X * Y):
         arrived(k).wait_send()
 
 
-def refine(rows, cols, ext, probe, meas, obj, probe_rows):
+def refine(counts, rows, cols, obj, probe, meas):
     forward, inverse = tables()
     whole = pl.BlockSpec(memory_space=pltpu.VMEM)
     scalars = pl.BlockSpec(memory_space=pltpu.SMEM)
+    remote = pl.BlockSpec(memory_space=pl.ANY)
     return pl.pallas_call(
         refine_kernel,
         out_shape=(
             jax.ShapeDtypeStruct((2, 128, 512), f32), jax.ShapeDtypeStruct((4, 4, N), f32)
         ),
-        in_specs=[scalars] * 2 + [whole] * 7,
+        in_specs=[scalars] * 3 + [remote] * 5,
         out_specs=(whole, whole),
         scratch_shapes=[
+            pltpu.VMEM((2, 128, 512), f32),
+            pltpu.VMEM((2, 2, N, N), f32),
+            pltpu.VMEM((3, N, N), f32),
+            pltpu.VMEM((2 * N, 2 * N), bf),
+            pltpu.VMEM((2 * N, 2 * N), bf),
+            pltpu.VMEM((2, 128, 512), bf),
+            pltpu.VMEM((2, 512, 768), bf),
+            pltpu.VMEM((4, 4, N, N), bf),
+            pltpu.VMEM((3, N, N), f32),
             pltpu.VMEM((3, 2, N, N), f32),
             pltpu.VMEM((3, N, N), f32),
             pltpu.VMEM((3, 8, 2 * N, N), f32),
@@ -458,26 +472,18 @@
             pltpu.VMEM((2, 128, 512), bf),
             pltpu.VMEM((2, 2, 128, 128), bf),
             pltpu.VMEM((4, 2, 128, 128), bf),
-            pltpu.SemaphoreType.DMA((40,)), pltpu.SemaphoreType.DMA((40,)),
+            pltpu.SemaphoreType.DMA((60,)), pltpu.SemaphoreType.DMA((60,)),
+            pltpu.SemaphoreType.DMA((5,)),
         ],
         compiler_params=pltpu.CompilerParams(
             collective_id=1, has_side_effects=True, vmem_limit_bytes=60 * 2**20
         ),
         name="refine",
-    )(rows, cols, ext, probe, meas, jnp.asarray(forward), jnp.asarray(inverse), obj, probe_rows)
+    )(counts, rows, cols, obj, probe, meas, jnp.asarray(forward), jnp.asarray(inverse))
 
 
 def local(object_field, probe, measured, scan_rows, scan_cols, counts):
-    slots = scan_rows.shape[0]
-    first_slot = lax.axis_index("mode") * slots
-    live = first_slot + jnp.arange(slots, dtype=jnp.int32) < counts[0]
-    live_rows = jnp.where(live, scan_rows, 4096)
-    extended, probe_all = gather(object_field, probe)
-    probe_rows = lax.dynamic_slice_in_dim(probe, lax.axis_index("tile") * 4, 4, 2)
-    object_out, probe_out = refine(
-        live_rows, scan_cols, extended, probe_all, measured, object_field,
-        probe_rows.reshape(4, 4, N),
-    )
+    object_out, probe_out = refine(counts, scan_rows, scan_cols, object_field, probe, measured)
     return object_out, probe_out.reshape(2, 2, 4, N)
 
 

time: 108 us -> 91.3 us (0.85)
  Pallas kernels: 96 us -> 87.3 us
  local copies, waits for them, and re-layouts: 9.31 us -> 2.48 us
  other arithmetic: 1.17 us -> 0 us
    pallas_call x1 -> x0, Pallas kernels: 30.5 us -> none  [gather(): pl.pallas_call(gather_kernel, out_shape=(jax.ShapeDtypeStruct((2, 512, 76...]
    pallas_call x1, Pallas kernels: 65.4 us -> 87.3 us  [refine(): pl.pallas_call(refine_kernel, out_shape=(jax.ShapeDtypeStruct((2, 128, 51...]
    unnamed x10 -> x4, local copies, waits for them, and re-layouts: 7.95 us -> 2.48 us
    dynamic_slice x1 -> x0, local copies, waits for them, and re-layouts: 1.37 us -> none  [local(): lax.dynamic_slice_in_dim(probe, lax.axis_index('tile') * 4, 4, 2)]
    select_n x1 -> x0, other arithmetic: 1.17 us -> none  [local(): live_rows = jnp.where(live, scan_rows, 4096)]
where the time goes in v4:
time: 91.3 us; the launch traced here: 91.1 us
  Pallas kernels  87.3 us (96%)
  local copies, waits for them, and re-layouts  2.48 us (3%)
  between operations  1.3 us (1%)
    pallas_call x1, Pallas kernels, refine(): pl.pallas_call(refine_kernel, out_shape=(jax.ShapeDtypeStruct((2, 128, 51...  87.3 us
    unnamed x4, local copies, waits for them, and re-layouts  2.48 us

profile of v4, /device:TPU:6, one launch (start us, length us, event | category | flops | bytes accessed | tf_op | source)
XLA Modules:
  0.0 91.1 jit_solution(17406706543228076757)
XLA Ops:
  1.3 87.3 %refine.1 = (f32[2,128,512]{2,1,0:T(8,128)}, f32[4,4,256]{2,1,0:T(4,128)}) custom-call(s32[1]{0:T(128)S(6)} %copy.12.counts, s32[3]{0:T(128)} %rows_in.1, s32[3]{0:T(128)} %cols.1, f32[2,128,512]{2,1,0:T(8,128)} %obj_in.1, f32[2,2,256,256]{3,2,1,0:T(8,128)} %probe_in.1, f32[3,256,256]{2,1,0:T(8,128)} %meas_in.1, bf16[512,512]{1,0:T(8,128)(2,1)} %constant.4.clone.fwd_in, ...), custom_call_target="tpu_custom_call" | custom-call | tf_op jit(solution)/shard_map/refine/pallas_call | solution.py:429
  88.6 0.0 copy-start
  88.6 1.9 %copy.13 = f32[2,128,512]{2,1,0:T(8,128)} copy(f32[2,128,512]{2,1,0:T(8,128)} %get-tuple-element.8) | data formatting | bytes 1048576
  90.5 0.0 copy-done
  90.5 0.6 copy.14
Async XLA Ops:
  88.6 1.9 %copy-start = (f32[4,4,256]{2,1,0:T(4,128)S(1)}, f32[4,4,256]{2,1,0:T(4,128)}, u32[]{:S(2)}) copy-start(f32[4,4,256]{2,1,0:T(4,128)} %get-tuple-element.5) | copy-start | bytes 49156

commit v5 on v4

v5 whole, which is shorter than its diff:
```python
import functools

import jax
import jax.numpy as jnp
import ml_dtypes
import numpy as np
from jax import lax
from jax.experimental import pallas as pl
from jax.experimental.pallas import tpu as pltpu
from jax.sharding import PartitionSpec as P

object_reg = 0.5
probe_reg = 1.0
N = 256
H = N // 2
X, Y, Z = 4, 4, 8
bf = jnp.bfloat16
f32 = jnp.float32
MESH = pl.DeviceIdType.MESH


def tables():
    pos = np.arange(N)
    ang = (pos[:, None] * pos[None, :] % N) * (2.0 * np.pi / N)
    sc = 1.0 / np.sqrt(float(N))
    re = (np.cos(ang) * sc).astype(ml_dtypes.bfloat16)
    im = (-np.sin(ang) * sc).astype(ml_dtypes.bfloat16)
    out = []
    for p in range(2):
        c, s = re[:H, p::2], im[:H, p::2]
        out.append(np.block([[c, s], [-s, c]]))
    for p in range(2):
        c, s = re[p::2, :H], im[p::2, :H]
        out.append(np.block([[c, -s], [s, c]]))
    for p in range(2):
        c, s = re[:H, p::2], im[:H, p::2]
        out.append(np.block([[c, s], [-s, c]]))
    for p in range(2):
        c, s = re[p::2, :H], im[p::2, :H]
        out.append(np.block([[c, -s], [s, c]]))
    return np.stack(out).astype(ml_dtypes.bfloat16)


def side(parts):
    return jnp.concatenate(parts, 1)


def stack(parts):
    return jnp.concatenate(parts, 0)


def dot(a, b):
    return jnp.dot(a, b, preferred_element_type=f32)


def here():
    tile = lax.axis_index("tile")
    group = lax.axis_index("mode")
    x = (group // 2) * 2 + tile // (Y * Z)
    return tile, group, x, (tile // Z) % Y, tile % Z, group % 2


def device(x, y, z, core):
    return {"tile": (x % 2) * (Y * Z) + y * Z + z, "mode": (x // 2) * 2 + core}


def sender(send_sem, recv_sem):
    def make(index, src, dst, target):
        return pltpu.make_async_remote_copy(
            src_ref=src, dst_ref=dst, send_sem=send_sem.at[index], recv_sem=recv_sem.at[index],
            device_id=target, device_id_type=MESH,
        )
    return make


def refine_kernel(counts, rows_in, cols, obj_in, probe_in, meas_in, dft_in, object_out, probe_out,
                  obj, probe, meas, dft, block, ext, modes, powers,
                  from_cols, from_rows, to_rows, narrow, by, kept_light,
                  patch, factor, spec, light, terms, to_cols, total, grads,
                  out_probe, got_probe, out_power, got_power, pieces, got_y, whole_power, got_power_y,
                  wide, bands, got_z, rims, got_x, last_power, got_power_x,
                  out_light, got_light, far_light, far_got_light, halo_light, halo_got_light,
                  out_grad, got_grad, far_grad, far_got_grad, halo_grad, halo_got_grad,
                  send_sem, recv_sem, load_sem):
    loads = [
        pltpu.make_async_copy(src, dst, load_sem.at[i])
        for i, (src, dst) in enumerate(
            ((obj_in, obj), (probe_in, probe), (meas_in, meas), (dft_in, dft))
        )
    ]
    for load in loads:
        load.start()
    slots = 3
    tile, group, x, y, z, core = here()
    tiles = X * Y * Z // 2
    x_hi = group // 2
    sibling = device(x, y, z, 1 - core)
    opposite = device((x + 2) % X, y, z, core)
    before, after = (tile + tiles - 1) % tiles, (tile + 1) % tiles
    other = (group + 2) % 4
    halo_to = [
        {"tile": before, "mode": group}, {"tile": before, "mode": other},
        {"tile": after, "mode": group}, {"tile": after, "mode": other},
    ]
    along_x = [device((x + i) % X, y, z, core) for i in (1, 3, 2)]
    along_z = [device(x, y, (z + i) % Z, core) for i in range(1, Z)]
    make = sender(send_sem, recv_sem)

    across = device(X - 1 - x, y, z, core)
    along_y = [device(x, (y + i) % Y, z, core) for i in (1, 3, 2)]
    partners = [sibling] + halo_to + along_x + along_y + along_z
    barrier = pltpu.get_barrier_semaphore()
    for partner in partners:
        pl.semaphore_signal(barrier, inc=1, device_id=partner, device_id_type=MESH)
    rows = [jnp.where(group * slots + s < counts[0], rows_in[s], 4096) for s in range(slots)]

    mine = pl.multiple_of(group * 128, 128)
    theirs = pl.multiple_of(other * 128, 128)
    loads[0].wait()
    block[...] = obj[...].astype(bf)
    ext[:, pl.ds(mine, 128), 128:640] = block[...]

    @pl.when(tile == 0)
    def _():
        ext[:, :, :128] = jnp.zeros((2, 512, 128), bf)

    @pl.when(tile == tiles - 1)
    def _():
        ext[:, :, 640:] = jnp.zeros((2, 512, 128), bf)

    loads[1].wait()
    for k in range(2):
        for c in range(2):
            modes[group, 2 * k + c] = probe[k, c].astype(bf)
    pl.semaphore_wait(barrier, len(partners))

    def strip(start, low, width):
        return ext.at[:, pl.ds(start, 128), pl.ds(low, width)]

    def plane(which, index):
        return modes.at[which, pl.ds(index, 1)]

    cut = make(41, plane(group, y), plane(group, y), across)
    cut.start()
    own = make(47, modes.at[group], modes.at[group], sibling)
    own.start()
    far = make(40, block, strip(mine, 128, 512), opposite)
    far.start()
    left, right = block.at[:, :, pl.ds(0, 128)], block.at[:, :, pl.ds(384, 128)]
    halo = [
        make(42, left, strip(mine, 640, 128), halo_to[0]),
        make(43, left, strip(mine, 640, 128), halo_to[1]),
        make(44, right, strip(mine, 0, 128), halo_to[2]),
        make(45, right, strip(mine, 0, 128), halo_to[3]),
    ]
    sends = (tile > 0, tile > 0, tile < tiles - 1, tile < tiles - 1)
    gets = (tile < tiles - 1, tile < tiles - 1, tile > 0, tile > 0)
    for flag, copy in zip(sends, halo):
        pl.when(flag)(copy.start)
    near = make(46, block, strip(mine, 128, 512), sibling)
    near.start()

    def pass_on(index, ref):
        copy = make(index, ref, ref, sibling)
        copy.start()
        return copy

    def picks(height, width, shift, down):
        high = lax.broadcasted_iota(jnp.int32, (height, width), 0)
        wide = lax.broadcasted_iota(jnp.int32, (height, width), 1)
        hit = high == wide + shift if down else wide == high + shift
        return jnp.where(hit, 1.0, 0.0).astype(bf)

    def sorted_by_parity(down):
        high = lax.broadcasted_iota(jnp.int32, (N, N), 0)
        wide = lax.broadcasted_iota(jnp.int32, (N, N), 1)
        place, held = (high, wide) if down else (wide, high)
        hit = held == jnp.where(place < N // 2, 2 * place, 2 * place - (N - 1))
        return jnp.where(hit, 1.0, 0.0).astype(f32)

    for s in range(slots):
        from_cols[s] = picks(768, N, cols[s], True)
        from_rows[s] = picks(N, 512, rows[s], False)
        to_rows[s] = picks(512, N, rows[s], True)
        to_cols[s * N:(s + 1) * N, :] = picks(N, 768, cols[s], False)
    light[...] = jnp.zeros_like(light)
    wide[...] = jnp.zeros_like(wide)
    powers[...] = jnp.zeros_like(powers)
    grads[...] = jnp.zeros_like(grads)
    loads[2].wait()
    for s in range(slots):
        by_cols = jnp.dot(meas[s], sorted_by_parity(False), precision=lax.Precision.HIGHEST,
                          preferred_element_type=f32)
        meas[s] = jnp.dot(sorted_by_parity(True), by_cols, precision=lax.Precision.HIGHEST,
                          preferred_element_type=f32)

    def scatter(c):
        spread_rows = [dot(to_rows[s], terms[s]).astype(bf) for s in range(slots)]
        total[c] = dot(jnp.concatenate(spread_rows, 1), to_cols[...])

    def sibling_rows(c, out, k):
        for h in range(2):
            start = pl.multiple_of((2 * h + 1 - core) * 128, 128)
            out[h, k] = total[c, pl.ds(start, 128), :].astype(bf)

    def own_rows(c, h, got, k):
        start = pl.multiple_of((2 * h + core) * 128, 128)
        return total[c, pl.ds(start, 128), :] + got[h, k].astype(f32)

    def fan_out(first, far, far_got, halo, halo_got):
        copies = [
            make(first, far.at[:, :, pl.ds(128, 512)], far_got, opposite),
            make(first + 1, halo.at[0], halo_got.at[0], halo_to[0]),
            make(first + 2, far.at[:, :, pl.ds(0, 128)], halo_got.at[1], halo_to[1]),
            make(first + 3, halo.at[1], halo_got.at[2], halo_to[2]),
            make(first + 4, far.at[:, :, pl.ds(640, 128)], halo_got.at[3], halo_to[3]),
        ]
        for copy in copies:
            copy.start()
        return copies

    keep_left = jnp.where(tile > 0, 1.0, 0.0)
    keep_right = jnp.where(tile < tiles - 1, 1.0, 0.0)

    def merged(kept, far_got, halo_got, k):
        center = kept[:, 128:640] + far_got[k].astype(f32)
        from_right = (halo_got[0, k].astype(f32) + halo_got[1, k].astype(f32)) * keep_right
        from_left = (halo_got[2, k].astype(f32) + halo_got[3, k].astype(f32)) * keep_left
        return jnp.concatenate(
            [center[:, :128] + from_left, center[:, 128:384], center[:, 384:] + from_right], 1
        )

    cut.wait_recv()
    around = []
    for i, target in enumerate(along_y):
        copy = make(48 + i, plane(other, y), plane(other, y), target)
        copy.start()
        around.append(copy)
    planes_on = [pass_on(51, plane(other, y))]

    def narrow_rows(which):
        start = pl.multiple_of(which * 128, 128)
        for s in range(slots):
            for c in range(2):
                narrow[s, c, pl.ds(start, 128), :] = dot(
                    ext[c, pl.ds(start, 128), :], from_cols[s]
                ).astype(bf)

    halo_kept = []
    for i, (flag, start, low) in enumerate(
        zip(gets, (mine, theirs, mine, theirs), (640, 640, 0, 0))
    ):
        halo_kept.append((flag, make(52 + i, strip(start, low, 128), strip(start, low, 128), sibling)))

    def halo_on(i):
        flag, on = halo_kept[i]

        @pl.when(flag)
        def _():
            halo[i].wait_recv()
            on.start()

    def halo_in(i):
        flag, on = halo_kept[i]
        pl.when(flag)(on.wait_recv)

    halo_on(0)
    halo_on(2)
    narrow_rows(group)
    near.wait_recv()
    halo_in(0)
    halo_in(2)
    narrow_rows(group + 1 - 2 * core)
    for i, step in enumerate((1, 3, 2)):
        around[i].wait_recv()
        planes_on.append(pass_on(57 + i, plane(other, (y + Y - step) % Y)))
    halo_on(1)
    halo_on(3)
    far.wait_recv()
    far_on = pass_on(56, strip(theirs, 128, 512))
    narrow_rows(other)
    own.wait_recv()
    for copy in planes_on:
        copy.wait_recv()
    def mode_light(g, _):
        for k in range(2):
            re = modes[g, 2 * k].astype(f32)
            im = modes[g, 2 * k + 1].astype(f32)
            light[...] += re * re + im * im
        return 0
    lax.fori_loop(0, 4, mode_light, 0)

    for s in range(slots):
        terms[s] = light[...].astype(bf)
    scatter(0)
    sibling_rows(0, out_light, 0)
    light_copy = make(1, out_light, got_light, sibling)
    light_copy.start()
    far_on.wait_recv()
    halo_in(1)
    halo_in(3)
    narrow_rows((other // 2) * 2 + 1 - core)
    for s in range(slots):
        for c in range(2):
            patch[s, c] = dot(from_rows[s], narrow[s, c])
    factor[0] = patch[0, 0] * patch[0, 0] + patch[0, 1] * patch[0, 1]
    for s in range(1, slots):
        factor[0] += patch[s, 0] * patch[s, 0] + patch[s, 1] * patch[s, 1]
    out_power[...] = factor[0].astype(bf)
    power_copy = make(0, out_power, got_power, sibling)
    power_copy.start()
    loads[3].wait()
    light_copy.wait_recv()
    kept = own_rows(0, x_hi, got_light, 0)
    kept_light[...] = kept
    far_light[0] = own_rows(0, 1 - x_hi, got_light, 0).astype(bf)
    halo_light[0, 0] = kept[:, :128].astype(bf)
    halo_light[1, 0] = kept[:, 640:].astype(bf)
    light_copies = fan_out(2, far_light, far_got_light, halo_light, halo_got_light)

    def spectra(m, _):
        pr = modes[m // 2, 2 * (m % 2)].astype(f32)
        pi = modes[m // 2, 2 * (m % 2) + 1].astype(f32)
        added, taken = [], []
        for s in range(slots):
            re = pr * patch[s, 0] - pi * patch[s, 1]
            im = pr * patch[s, 1] + pi * patch[s, 0]
            added.append(side([re[:, :H] + re[:, H:], im[:, :H] + im[:, H:]]).astype(bf))
            taken.append(side([re[:, :H] - re[:, H:], im[:, :H] - im[:, H:]]).astype(bf))
        even = dot(stack(added), dft[0])
        odd = dot(stack(taken), dft[1])
        added, taken = [], []
        for s in range(slots):
            low, high = slice(s * N, s * N + H), slice(s * N + H, (s + 1) * N)
            e, o = even[low] + even[high], odd[low] + odd[high]
            added.append(stack([side([e[:, :H], o[:, :H]]), side([e[:, H:], o[:, H:]])]).astype(bf))
            e, o = even[low] - even[high], odd[low] - odd[high]
            taken.append(stack([side([e[:, :H], o[:, :H]]), side([e[:, H:], o[:, H:]])]).astype(bf))
        even = dot(dft[2], side(added))
        odd = dot(dft[3], side(taken))
        spec[m, :N] = even
        spec[m, N:] = odd
        for s in range(slots):
            e, o = even[:, s * N:(s + 1) * N], odd[:, s * N:(s + 1) * N]
            powers[s, :H] += e[:H] * e[:H] + e[H:] * e[H:]
            powers[s, H:] += o[:H] * o[:H] + o[H:] * o[H:]
        return 0
    lax.fori_loop(0, 8, spectra, 0, unroll=2)
    for s in range(slots):
        ratio = meas[s] * lax.rsqrt(jnp.maximum(powers[s], 0.25)) - 1.0
        for p in range(2):
            rows_p = ratio[p * H:(p + 1) * H]
            by[p, :, s * N:(s + 1) * N] = stack([rows_p, rows_p])


    def passed(i):
        return make(60 + i, out_probe.at[i], got_probe.at[i], sibling)

    def to_y(i, j):
        k = 3 * i + j - 1
        return make(70 + k, pieces.at[i, :, :, (y + j) % Y], got_y.at[k], device(x, (y + j) % Y, z, core))

    def power_y(j):
        return make(82 + j, whole_power.at[:, (y + j) % Y], got_power_y.at[j - 1],
                    device(x, (y + j) % Y, z, core))

    def to_z(h, i):
        height = 48 if h == 0 else 32
        return make(
            86 + 8 * h + i, bands.at[h, (z + i) % Z, pl.ds(0, height)],
            got_z.at[h, i, pl.ds(0, height)], along_z[i - 1]
        )

    def to_x(h, xl):
        i = (2 * h + xl - x + X) % X
        return make(104 + i, rims.at[h, pl.ds(16 * xl, 16)], got_x.at[i], device(2 * h + xl, y, z, core)), i

    def power_x(i):
        return make(108 + i, last_power.at[(x + i) % 2], got_power_x.at[i], device((x + i) % X, y, z, core))

    def reduce_y(h):
        for p in range(2):
            i = 2 * h + p
            band = pieces[i, :, :, y].astype(f32)
            for j in range(1, Y):
                to_y(i, j).wait_recv()
                band = band + got_y[3 * i + j - 1].astype(f32)
            for part in range(Z):
                for xl in range(2):
                    for c in range(2):
                        at = 16 * xl + 8 * p + 4 * c
                        wide[part, at:at + 4] = band[c, xl, 4 * part:4 * part + 4]
        if h == 0:
            band = whole_power[:, y].astype(f32)
            for j in range(1, Y):
                power_y(j).wait_recv()
                band = band + got_power_y[j - 1].astype(f32)
            for part in range(Z):
                for xl in range(2):
                    wide[part, 32 + 4 * xl:36 + 4 * xl] = band[xl, 4 * part:4 * part + 4]
        bands[h] = wide[...].astype(bf)
        for i in range(1, Z):
            to_z(h, i).start()

    def reduce_z(h):
        height = 48 if h == 0 else 32
        total_z = bands[h, z, :height].astype(f32)
        for i in range(1, Z):
            to_z(h, i).wait_recv()
            total_z = total_z + got_z[h, i, :height].astype(f32)
        rims[h] = total_z[:32]
        for xl in range(2):
            copy, i = to_x(h, xl)
            pl.when(i > 0)(copy.start)
        if h == 0:
            for xl in range(2):
                last_power[xl, :4] = total_z[32 + 4 * xl:36 + 4 * xl]
                last_power[xl, 4:] = total_z[36:40]
            for i in range(1, X):
                power_x(i).start()

    def back_step(step, _):
        i = step // 2
        m = 4 * (i // 2) + 2 * jnp.where(step % 2 == 0, 1 - core, core) + i % 2
        pr = modes[m // 2, 2 * (m % 2)].astype(f32)
        pi = modes[m // 2, 2 * (m % 2) + 1].astype(f32)
        even = dot(dft[4], (spec[m, :N] * by[0]).astype(bf))
        odd = dot(dft[5], (spec[m, N:] * by[1]).astype(bf))
        low, high = (even + odd).astype(bf), (even - odd).astype(bf)
        at_even, at_odd = [], []
        for s in range(slots):
            c, d = slice(s * N, s * N + H), slice(s * N + H, (s + 1) * N)
            at_even.append(side([stack([low[:H, c], high[:H, c]]), stack([low[H:, c], high[H:, c]])]))
            at_odd.append(side([stack([low[:H, d], high[:H, d]]), stack([low[H:, d], high[H:, d]])]))
        even = dot(stack(at_even), dft[6])
        odd = dot(stack(at_odd), dft[7])
        low, high = even + odd, even - odd
        sum_re, sum_im = None, None
        for s in range(slots):
            r = slice(s * N, (s + 1) * N)
            br = side([low[r, :H], high[r, :H]])
            bi = side([low[r, H:], high[r, H:]])
            ar = patch[s, 0]
            ai = patch[s, 1]
            re = ar * br + ai * bi
            im = ar * bi - ai * br
            sum_re = re if s == 0 else sum_re + re
            sum_im = im if s == 0 else sum_im + im
            grads[s, 0] += pr * br + pi * bi
            grads[s, 1] += pr * bi - pi * br

        @pl.when(step % 2 == 0)
        def _():
            out_probe[i, 0] = sum_re.astype(bf)
            out_probe[i, 1] = sum_im.astype(bf)
            passed(i).start()

        @pl.when(step % 2 == 1)
        def _():
            passed(i).wait_recv()
            for c, mine_sum in enumerate((sum_re, sum_im)):
                both = (mine_sum + got_probe[i, c].astype(f32)).astype(bf)
                pieces[i, c] = both.reshape(2, Y, 32, N)
            for j in range(1, Y):
                to_y(i, j).start()
        return 0

    power_copy.wait_recv()
    whole_power[...] = (out_power[...].astype(f32) + got_power[...].astype(f32)).astype(bf).reshape(2, Y, 32, N)
    for j in range(1, Y):
        power_y(j).start()
    lax.fori_loop(0, 8, back_step, 0)

    for copy in light_copies:
        copy.wait_recv()
    weight = merged(kept_light[...], far_got_light, halo_got_light, 0) + object_reg

    for c in range(2):
        for s in range(slots):
            terms[s] = grads[s, c].astype(bf)
        scatter(c)
    for c in range(2):
        sibling_rows(c, out_grad, c)
    grad_copy = make(32, out_grad, got_grad, sibling)
    grad_copy.start()
    reduce_y(0)
    grad_copy.wait_recv()
    for c in range(2):
        far_grad[c] = own_rows(c, 1 - x_hi, got_grad, c).astype(bf)
        halo_grad[0, c] = own_rows(c, x_hi, got_grad, c)[:, :128].astype(bf)
        halo_grad[1, c] = own_rows(c, x_hi, got_grad, c)[:, 640:].astype(bf)
    grad_copies = fan_out(33, far_grad, far_got_grad, halo_grad, halo_got_grad)

    reduce_y(1)
    reduce_z(0)
    reduce_z(1)
    for copy in grad_copies:
        copy.wait_recv()
    for c in range(2):
        kept = own_rows(c, x_hi, got_grad, c)
        object_out[c] = obj[c] + merged(kept, far_got_grad, halo_got_grad, c) / weight

    final = rims[x_hi, pl.ds(pl.multiple_of(16 * (x % 2), 16), 16)]
    weight = last_power[x % 2, :4] + probe_reg
    for i in range(1, X):
        make(104 + i, rims.at[0, pl.ds(0, 16)], got_x.at[i], sibling).wait_recv()
        final = final + got_x[i]
        power_x(i).wait_recv()
        weight = weight + got_power_x[i, :4]
    at = pl.multiple_of((tile // 2) * 8, 8)
    for k in range(4):
        rows8 = probe[k // 2, k % 2, pl.ds(at, 8), :]
        probe_row = jnp.where(tile % 2 == 0, rows8[:4], rows8[4:])
        probe_out[k] = probe_row + final[4 * k:4 * k + 4] / weight
    for copy in [far, cut, near, own, far_on] + around + planes_on:
        copy.wait_send()
    for flag, copy in zip(sends, halo):
        pl.when(flag)(copy.wait_send)
    for flag, copy in halo_kept:
        pl.when(flag)(copy.wait_send)
    for copy in [power_copy, light_copy, grad_copy, ] + light_copies + grad_copies:
        copy.wait_send()
    for i in range(4):
        passed(i).wait_send()
        for j in range(1, Y):
            to_y(i, j).wait_send()
    for h in range(2):
        for i in range(1, Z):
            to_z(h, i).wait_send()
    for j in range(1, Y):
        power_y(j).wait_send()
    for i in range(1, X):
        make(104 + i, rims.at[0, pl.ds(0, 16)], got_x.at[i], sibling).wait_send()
        power_x(i).wait_send()


def refine(counts, rows, cols, obj, probe, meas):
    whole = pl.BlockSpec(memory_space=pltpu.VMEM)
    scalars = pl.BlockSpec(memory_space=pltpu.SMEM)
    remote = pl.BlockSpec(memory_space=pl.ANY)
    return pl.pallas_call(
        refine_kernel,
        out_shape=(
            jax.ShapeDtypeStruct((2, 128, 512), f32), jax.ShapeDtypeStruct((4, 4, N), f32)
        ),
        in_specs=[scalars] * 3 + [remote] * 4,
        out_specs=(whole, whole),
        scratch_shapes=[
            pltpu.VMEM((2, 128, 512), f32),
            pltpu.VMEM((2, 2, N, N), f32),
            pltpu.VMEM((3, N, N), f32),
            pltpu.VMEM((8, N, N), bf),
            pltpu.VMEM((2, 128, 512), bf),
            pltpu.VMEM((2, 512, 768), bf),
            pltpu.VMEM((4, 4, N, N), bf),
            pltpu.VMEM((3, N, N), f32),
            pltpu.VMEM((3, 768, N), bf),
            pltpu.VMEM((3, N, 512), bf),
            pltpu.VMEM((3, 512, N), bf),
            pltpu.VMEM((3, 2, 512, N), bf),
            pltpu.VMEM((2, N, 3 * N), f32),
            pltpu.VMEM((128, 768), f32),
            pltpu.VMEM((3, 2, N, N), f32),
            pltpu.VMEM((3, N, N), f32),
            pltpu.VMEM((8, 2 * N, 3 * N), f32),
            pltpu.VMEM((N, N), f32),
            pltpu.VMEM((3, N, N), bf),
            pltpu.VMEM((3 * N, 768), bf),
            pltpu.VMEM((2, 512, 768), f32),
            pltpu.VMEM((3, 2, N, N), f32),
            pltpu.VMEM((4, 2, N, N), bf),
            pltpu.VMEM((4, 2, N, N), bf),
            pltpu.VMEM((N, N), bf),
            pltpu.VMEM((N, N), bf),
            pltpu.VMEM((4, 2, 2, Y, 32, N), bf),
            pltpu.VMEM((12, 2, 2, 32, N), bf),
            pltpu.VMEM((2, Y, 32, N), bf),
            pltpu.VMEM((3, 2, 32, N), bf),
            pltpu.VMEM((Z, 48, N), f32),
            pltpu.VMEM((2, Z, 48, N), bf),
            pltpu.VMEM((2, Z, 48, N), bf),
            pltpu.VMEM((2, 32, N), f32),
            pltpu.VMEM((X, 16, N), f32),
            pltpu.VMEM((2, 8, N), f32),
            pltpu.VMEM((X, 8, N), f32),
            pltpu.VMEM((2, 1, 128, 768), bf),
            pltpu.VMEM((2, 1, 128, 768), bf),
            pltpu.VMEM((1, 128, 768), bf),
            pltpu.VMEM((1, 128, 512), bf),
            pltpu.VMEM((2, 1, 128, 128), bf),
            pltpu.VMEM((4, 1, 128, 128), bf),
            pltpu.VMEM((2, 2, 128, 768), bf),
            pltpu.VMEM((2, 2, 128, 768), bf),
            pltpu.VMEM((2, 128, 768), bf),
            pltpu.VMEM((2, 128, 512), bf),
            pltpu.VMEM((2, 2, 128, 128), bf),
            pltpu.VMEM((4, 2, 128, 128), bf),
            pltpu.SemaphoreType.DMA((112,)), pltpu.SemaphoreType.DMA((112,)),
            pltpu.SemaphoreType.DMA((4,)),
        ],
        compiler_params=pltpu.CompilerParams(
            collective_id=1, has_side_effects=True, vmem_limit_bytes=60 * 2**20
        ),
        name="refine",
    )(counts, rows, cols, obj, probe, meas, jnp.asarray(tables()))


def local(object_field, probe, measured, scan_rows, scan_cols, counts):
    object_out, probe_out = refine(counts, scan_rows, scan_cols, object_field, probe, measured)
    return object_out, probe_out.reshape(2, 2, 4, N)


def solution(mesh):
    return jax.shard_map(
        local,
        mesh=mesh,
        in_specs=(
            P(None, "mode", "tile"),
            P("mode", None, None, None),
            P(("tile", "mode"), None, None),
            P(("tile", "mode")),
            P(("tile", "mode")),
            P("tile"),
        ),
        out_specs=(P(None, "mode", "tile"), P("mode", None, "tile", None)),
        check_vma=False,
    )
```

time: 91.3 us -> 75.1 us (0.82)
  Pallas kernels: 87.3 us -> 70.7 us
    pallas_call x1, Pallas kernels: 87.3 us -> 70.7 us  [refine(): pl.pallas_call(refine_kernel, out_shape=(jax.ShapeDtypeStruct((2, 128, 51...]
where the time goes in v5:
time: 75.1 us; the launch traced here: 74.5 us
  Pallas kernels  70.7 us (94%)
  local copies, waits for them, and re-layouts  2.48 us (3%)
  between operations  1.29 us (2%)
    pallas_call x1, Pallas kernels, refine(): pl.pallas_call(refine_kernel, out_shape=(jax.ShapeDtypeStruct((2, 128, 51...  70.7 us
    unnamed x4, local copies, waits for them, and re-layouts  2.48 us

profile of v5, /device:TPU:6, one launch (start us, length us, event | category | flops | bytes accessed | tf_op | source)
XLA Modules:
  0.0 74.5 jit_solution(12664911284393597576)
XLA Ops:
  1.3 70.7 %refine.1 = (f32[2,128,512]{2,1,0:T(8,128)}, f32[4,4,256]{2,1,0:T(4,128)}) custom-call(s32[1]{0:T(128)S(6)} %copy.11.counts, s32[3]{0:T(128)} %rows_in.1, s32[3]{0:T(128)} %cols.1, f32[2,128,512]{2,1,0:T(8,128)} %obj_in.1, f32[2,2,256,256]{3,2,1,0:T(8,128)} %probe_in.1, f32[3,256,256]{2,1,0:T(8,128)} %meas_in.1, bf16[8,256,256]{2,1,0:T(8,128)(2,1)} %constant.2.clone.dft_in), custom_call_target="tpu_custom_call" | custom-call | tf_op jit(solution)/shard_map/refine/pallas_call | solution.py:541
  72.0 0.0 copy-start
  72.0 1.9 %copy.12 = f32[2,128,512]{2,1,0:T(8,128)} copy(f32[2,128,512]{2,1,0:T(8,128)} %get-tuple-element.8) | data formatting | bytes 1048576
  73.9 0.0 copy-done
  73.9 0.6 copy.13
Async XLA Ops:
  72.0 1.9 %copy-start = (f32[4,4,256]{2,1,0:T(4,128)S(1)}, f32[4,4,256]{2,1,0:T(4,128)}, u32[]{:S(2)}) copy-start(f32[4,4,256]{2,1,0:T(4,128)} %get-tuple-element.5) | copy-start | bytes 49156

commit v6 on v5

--- a/solution.py
+++ b/solution.py
@@ -271,31 +271,11 @@
     halo_in(0)
     halo_in(2)
     narrow_rows(group + 1 - 2 * core)
-    for i, step in enumerate((1, 3, 2)):
-        around[i].wait_recv()
-        planes_on.append(pass_on(57 + i, plane(other, (y + Y - step) % Y)))
     halo_on(1)
     halo_on(3)
     far.wait_recv()
     far_on = pass_on(56, strip(theirs, 128, 512))
     narrow_rows(other)
-    own.wait_recv()
-    for copy in planes_on:
-        copy.wait_recv()
-    def mode_light(g, _):
-        for k in range(2):
-            re = modes[g, 2 * k].astype(f32)
-            im = modes[g, 2 * k + 1].astype(f32)
-            light[...] += re * re + im * im
-        return 0
-    lax.fori_loop(0, 4, mode_light, 0)
-
-    for s in range(slots):
-        terms[s] = light[...].astype(bf)
-    scatter(0)
-    sibling_rows(0, out_light, 0)
-    light_copy = make(1, out_light, got_light, sibling)
-    light_copy.start()
     far_on.wait_recv()
     halo_in(1)
     halo_in(3)
@@ -310,15 +290,9 @@
     power_copy = make(0, out_power, got_power, sibling)
     power_copy.start()
     loads[3].wait()
-    light_copy.wait_recv()
-    kept = own_rows(0, x_hi, got_light, 0)
-    kept_light[...] = kept
-    far_light[0] = own_rows(0, 1 - x_hi, got_light, 0).astype(bf)
-    halo_light[0, 0] = kept[:, :128].astype(bf)
-    halo_light[1, 0] = kept[:, 640:].astype(bf)
-    light_copies = fan_out(2, far_light, far_got_light, halo_light, halo_got_light)
-
-    def spectra(m, _):
+
+    def spectra(q, g):
+        m = 2 * g + q
         pr = modes[m // 2, 2 * (m % 2)].astype(f32)
         pi = modes[m // 2, 2 * (m % 2) + 1].astype(f32)
         added, taken = [], []
@@ -344,8 +318,35 @@
             e, o = even[:, s * N:(s + 1) * N], odd[:, s * N:(s + 1) * N]
             powers[s, :H] += e[:H] * e[:H] + e[H:] * e[H:]
             powers[s, H:] += o[:H] * o[:H] + o[H:] * o[H:]
-        return 0
-    lax.fori_loop(0, 8, spectra, 0, unroll=2)
+        return g
+
+    def mode_light(g):
+        for k in range(2):
+            re = modes[g, 2 * k].astype(f32)
+            im = modes[g, 2 * k + 1].astype(f32)
+            light[...] += re * re + im * im
+
+    near_group = group + 1 - 2 * core
+    lax.fori_loop(0, 2, spectra, group, unroll=True)
+    for i, step in enumerate((1, 3, 2)):
+        around[i].wait_recv()
+        planes_on.append(pass_on(57 + i, plane(other, (y + Y - step) % Y)))
+    own.wait_recv()
+    lax.fori_loop(0, 2, spectra, near_group, unroll=True)
+    mode_light(group)
+    mode_light(near_group)
+    for copy in planes_on:
+        copy.wait_recv()
+    lax.fori_loop(0, 2, spectra, other, unroll=True)
+    lax.fori_loop(0, 2, spectra, (near_group + 2) % 4, unroll=True)
+    mode_light(other)
+    mode_light((near_group + 2) % 4)
+    for s in range(slots):
+        terms[s] = light[...].astype(bf)
+    scatter(0)
+    sibling_rows(0, out_light, 0)
+    light_copy = make(1, out_light, got_light, sibling)
+    light_copy.start()
     for s in range(slots):
         ratio = meas[s] * lax.rsqrt(jnp.maximum(powers[s], 0.25)) - 1.0
         for p in range(2):
@@ -469,7 +470,15 @@
     whole_power[...] = (out_power[...].astype(f32) + got_power[...].astype(f32)).astype(bf).reshape(2, Y, 32, N)
     for j in range(1, Y):
         power_y(j).start()
-    lax.fori_loop(0, 8, back_step, 0)
+    lax.fori_loop(0, 2, back_step, 0)
+    light_copy.wait_recv()
+    kept = own_rows(0, x_hi, got_light, 0)
+    kept_light[...] = kept
+    far_light[0] = own_rows(0, 1 - x_hi, got_light, 0).astype(bf)
+    halo_light[0, 0] = kept[:, :128].astype(bf)
+    halo_light[1, 0] = kept[:, 640:].astype(bf)
+    light_copies = fan_out(2, far_light, far_got_light, halo_light, halo_got_light)
+    lax.fori_loop(2, 8, back_step, 0)
 
     for copy in light_copies:
         copy.wait_recv()

time: 75.1 us -> 72.1 us (0.960)
  Pallas kernels: 70.7 us -> 67.6 us
    pallas_call x1, Pallas kernels: 70.7 us -> 67.6 us  [refine(): pl.pallas_call(refine_kernel, out_shape=(jax.ShapeDtypeStruct((2, 128, 51...]
where the time goes in v6:
time: 72.1 us; the launch traced here: 71.3 us
  Pallas kernels  67.6 us (94%)
  local copies, waits for them, and re-layouts  2.48 us (3%)
  between operations  1.3 us (2%)
    pallas_call x1, Pallas kernels, refine(): pl.pallas_call(refine_kernel, out_shape=(jax.ShapeDtypeStruct((2, 128, 51...  67.6 us
    unnamed x4, local copies, waits for them, and re-layouts  2.48 us

profile of v6, /device:TPU:6, one launch (start us, length us, event | category | flops | bytes accessed | tf_op | source)
XLA Modules:
  0.0 71.3 jit_solution(3929220020323603310)
XLA Ops:
  1.3 67.6 %refine.1 = (f32[2,128,512]{2,1,0:T(8,128)}, f32[4,4,256]{2,1,0:T(4,128)}) custom-call(s32[1]{0:T(128)S(6)} %copy.11.counts, s32[3]{0:T(128)} %rows_in.1, s32[3]{0:T(128)} %cols.1, f32[2,128,512]{2,1,0:T(8,128)} %obj_in.1, f32[2,2,256,256]{3,2,1,0:T(8,128)} %probe_in.1, f32[3,256,256]{2,1,0:T(8,128)} %meas_in.1, bf16[8,256,256]{2,1,0:T(8,128)(2,1)} %constant.2.clone.dft_in), custom_call_target="tpu_custom_call" | custom-call | tf_op jit(solution)/shard_map/refine/pallas_call | solution.py:550
  68.8 0.0 copy-start
  68.9 1.9 %copy.12 = f32[2,128,512]{2,1,0:T(8,128)} copy(f32[2,128,512]{2,1,0:T(8,128)} %get-tuple-element.8) | data formatting | bytes 1048576
  70.7 0.0 copy-done
  70.7 0.6 copy.13
Async XLA Ops:
  68.8 1.9 %copy-start = (f32[4,4,256]{2,1,0:T(4,128)S(1)}, f32[4,4,256]{2,1,0:T(4,128)}, u32[]{:S(2)}) copy-start(f32[4,4,256]{2,1,0:T(4,128)} %get-tuple-element.5) | copy-start | bytes 49156

commit v7 on v6

--- a/solution.py
+++ b/solution.py
@@ -107,7 +107,7 @@
     make = sender(send_sem, recv_sem)
 
     across = device(X - 1 - x, y, z, core)
-    along_y = [device(x, (y + i) % Y, z, core) for i in (1, 3, 2)]
+    along_y = [device(x, (y + i) % Y, z, core) for i in (2, 1, 3)]
     partners = [sibling] + halo_to + along_x + along_y + along_z
     barrier = pltpu.get_barrier_semaphore()
     for partner in partners:
@@ -155,8 +155,8 @@
     ]
     sends = (tile > 0, tile > 0, tile < tiles - 1, tile < tiles - 1)
     gets = (tile < tiles - 1, tile < tiles - 1, tile > 0, tile > 0)
-    for flag, copy in zip(sends, halo):
-        pl.when(flag)(copy.start)
+    for i in (1, 3, 0, 2):
+        pl.when(sends[i])(halo[i].start)
     near = make(46, block, strip(mine, 128, 512), sibling)
     near.start()
 
@@ -328,7 +328,7 @@
 
     near_group = group + 1 - 2 * core
     lax.fori_loop(0, 2, spectra, group, unroll=True)
-    for i, step in enumerate((1, 3, 2)):
+    for i, step in enumerate((2, 1, 3)):
         around[i].wait_recv()
         planes_on.append(pass_on(57 + i, plane(other, (y + Y - step) % Y)))
     own.wait_recv()
@@ -400,7 +400,7 @@
                 for xl in range(2):
                     wide[part, 32 + 4 * xl:36 + 4 * xl] = band[xl, 4 * part:4 * part + 4]
         bands[h] = wide[...].astype(bf)
-        for i in range(1, Z):
+        for i in (4, 3, 5, 2, 6, 1, 7):
             to_z(h, i).start()
 
     def reduce_z(h):
@@ -462,7 +462,7 @@
             for c, mine_sum in enumerate((sum_re, sum_im)):
                 both = (mine_sum + got_probe[i, c].astype(f32)).astype(bf)
                 pieces[i, c] = both.reshape(2, Y, 32, N)
-            for j in range(1, Y):
+            for j in (2, 1, 3):
                 to_y(i, j).start()
         return 0
 

time: 72.1 us -> 71 us (0.985)
  no operation moved by 1% of the time
where the time goes in v7:
time: 71 us; the launch traced here: 70.9 us
  Pallas kernels  67.1 us (95%)
  local copies, waits for them, and re-layouts  2.48 us (3%)
  between operations  1.3 us (2%)
    pallas_call x1, Pallas kernels, refine(): pl.pallas_call(refine_kernel, out_shape=(jax.ShapeDtypeStruct((2, 128, 51...  67.1 us
    unnamed x4, local copies, waits for them, and re-layouts  2.48 us

profile of v7, /device:TPU:6, one launch (start us, length us, event | category | flops | bytes accessed | tf_op | source)
XLA Modules:
  0.0 70.9 jit_solution(15356583389102213440)
XLA Ops:
  1.3 67.1 %refine.1 = (f32[2,128,512]{2,1,0:T(8,128)}, f32[4,4,256]{2,1,0:T(4,128)}) custom-call(s32[1]{0:T(128)S(6)} %copy.11.counts, s32[3]{0:T(128)} %rows_in.1, s32[3]{0:T(128)} %cols.1, f32[2,128,512]{2,1,0:T(8,128)} %obj_in.1, f32[2,2,256,256]{3,2,1,0:T(8,128)} %probe_in.1, f32[3,256,256]{2,1,0:T(8,128)} %meas_in.1, bf16[8,256,256]{2,1,0:T(8,128)(2,1)} %constant.2.clone.dft_in), custom_call_target="tpu_custom_call" | custom-call | tf_op jit(solution)/shard_map/refine/pallas_call | solution.py:550
  68.4 0.0 copy-start
  68.4 1.9 %copy.12 = f32[2,128,512]{2,1,0:T(8,128)} copy(f32[2,128,512]{2,1,0:T(8,128)} %get-tuple-element.8) | data formatting | bytes 1048576
  70.3 0.0 copy-done
  70.3 0.6 copy.13
Async XLA Ops:
  68.4 1.9 %copy-start = (f32[4,4,256]{2,1,0:T(4,128)S(1)}, f32[4,4,256]{2,1,0:T(4,128)}, u32[]{:S(2)}) copy-start(f32[4,4,256]{2,1,0:T(4,128)} %get-tuple-element.5) | copy-start | bytes 49156

commit v8 on v7

--- a/solution.py
+++ b/solution.py
@@ -215,8 +215,8 @@
             make(first + 3, halo.at[1], halo_got.at[2], halo_to[2]),
             make(first + 4, far.at[:, :, pl.ds(640, 128)], halo_got.at[3], halo_to[3]),
         ]
-        for copy in copies:
-            copy.start()
+        for i in (2, 4, 0, 1, 3):
+            copies[i].start()
         return copies
 
     keep_left = jnp.where(tile > 0, 1.0, 0.0)
@@ -492,7 +492,6 @@
         sibling_rows(c, out_grad, c)
     grad_copy = make(32, out_grad, got_grad, sibling)
     grad_copy.start()
-    reduce_y(0)
     grad_copy.wait_recv()
     for c in range(2):
         far_grad[c] = own_rows(c, 1 - x_hi, got_grad, c).astype(bf)
@@ -500,6 +499,7 @@
         halo_grad[1, c] = own_rows(c, x_hi, got_grad, c)[:, 640:].astype(bf)
     grad_copies = fan_out(33, far_grad, far_got_grad, halo_grad, halo_got_grad)
 
+    reduce_y(0)
     reduce_y(1)
     reduce_z(0)
     reduce_z(1)

time: 71 us -> 73.6 us (1.037)
  Pallas kernels: 67.1 us -> 69.6 us
    pallas_call x1, Pallas kernels: 67.1 us -> 69.6 us  [refine(): pl.pallas_call(refine_kernel, out_shape=(jax.ShapeDtypeStruct((2, 128, 51...]
where the time goes in v8:
time: 73.6 us; the launch traced here: 73.4 us
  Pallas kernels  69.6 us (95%)
  local copies, waits for them, and re-layouts  2.48 us (3%)
  between operations  1.3 us (2%)
    pallas_call x1, Pallas kernels, refine(): pl.pallas_call(refine_kernel, out_shape=(jax.ShapeDtypeStruct((2, 128, 51...  69.6 us
    unnamed x4, local copies, waits for them, and re-layouts  2.48 us

profile of v8, /device:TPU:6, one launch (start us, length us, event | category | flops | bytes accessed | tf_op | source)
XLA Modules:
  0.0 73.4 jit_solution(4243425443279331939)
XLA Ops:
  1.3 69.6 %refine.1 = (f32[2,128,512]{2,1,0:T(8,128)}, f32[4,4,256]{2,1,0:T(4,128)}) custom-call(s32[1]{0:T(128)S(6)} %copy.11.counts, s32[3]{0:T(128)} %rows_in.1, s32[3]{0:T(128)} %cols.1, f32[2,128,512]{2,1,0:T(8,128)} %obj_in.1, f32[2,2,256,256]{3,2,1,0:T(8,128)} %probe_in.1, f32[3,256,256]{2,1,0:T(8,128)} %meas_in.1, bf16[8,256,256]{2,1,0:T(8,128)(2,1)} %constant.2.clone.dft_in), custom_call_target="tpu_custom_call" | custom-call | tf_op jit(solution)/shard_map/refine/pallas_call | solution.py:550
  70.9 0.0 copy-start
  70.9 1.9 %copy.12 = f32[2,128,512]{2,1,0:T(8,128)} copy(f32[2,128,512]{2,1,0:T(8,128)} %get-tuple-element.8) | data formatting | bytes 1048576
  72.8 0.0 copy-done
  72.8 0.6 copy.13
Async XLA Ops:
  70.9 1.9 %copy-start = (f32[4,4,256]{2,1,0:T(4,128)S(1)}, f32[4,4,256]{2,1,0:T(4,128)}, u32[]{:S(2)}) copy-start(f32[4,4,256]{2,1,0:T(4,128)} %get-tuple-element.5) | copy-start | bytes 49156
